TPU v7x, 256 devices: a whole 4x4x8 slice. The times are simulated.
256 devices in a mesh: tblk: 2 (over y_hi), chan: 128 (over y_lo, z, x, core).
Axes of the slice: x: 4, y: 4 (y_hi: 2, y_lo: 2; y = y_hi * 2 + y_lo), z: 8, core: 2. Of those that a mesh axis runs over, the one named last changes fastest.
Arguments:
- voltages: bfloat16 [8, 2, 1024, 32768], P(None, 'tblk', 'chan'), may hold values from -9 to 9
- input_gains: float32 [1024], P('chan'), may hold values from 0.5 to 2
Outputs:
- visibilities: bfloat16 [512, 2, 1024, 1024], P(('tblk', 'chan'))
All inputs are finite; a program needn't handle non-finite values.
Results may differ from a plain program's by a relative error of at most 0.0054.
Values may be sent and summed in bfloat16 or wider, within the bound.
No kernel may reach another device: no remote copies, remote signals or barrier semaphores. Data moves between devices by JAX's collectives and lax.ppermute only.
A program may use at most 128 MiB of HBM per device.

v0:
```python
import math

import jax
import jax.numpy as jnp
from jax import lax
from jax.sharding import PartitionSpec as P

CHANNELS = 512
NFFT = 2048
TAPS = 4
SPEC = 16


def from_behind(block, axis, distance):
    devices = range(lax.axis_size(axis))
    route = [((i - distance) % len(devices), i) for i in devices]
    return lax.ppermute(block, axis, route)


def prototype(tap_count, fft_len):
    positions = jnp.arange(tap_count * fft_len, dtype=jnp.float32) + 0.5
    window = 0.5 - 0.5 * jnp.cos(2.0 * math.pi * positions / (tap_count * fft_len))
    shape_fn = jnp.sinc(positions / fft_len - tap_count / 2.0) * window
    shape_fn = shape_fn / jnp.sqrt(tap_count * jnp.mean(shape_fn * shape_fn))
    return shape_fn.reshape(tap_count, fft_len)


def make_table(chan_count, fft_len):
    chan_ids = jnp.arange(chan_count, dtype=jnp.int32)
    sample_ids = jnp.arange(fft_len, dtype=jnp.int32)
    phase = chan_ids[:, None] * sample_ids[None, :] % fft_len
    phase_angle = phase.astype(jnp.float32) * (2.0 * math.pi / fft_len)
    norm_scale = 1.0 / math.sqrt(fft_len)
    stacked = jnp.stack(
        [jnp.cos(phase_angle) * norm_scale, -jnp.sin(phase_angle) * norm_scale], axis=1
    )
    return stacked.astype(jnp.bfloat16)


def products(left_side, right_side):
    return lax.dot_general(
        left_side, right_side, (((1,), (1,)), ((), ())), preferred_element_type=jnp.float32
    )


def hermitian(left_rows, swapped, norm_scale):
    real_part = products(left_rows, left_rows)
    imag_part = products(swapped, left_rows)
    return (jnp.stack([real_part, imag_part]) * norm_scale).astype(jnp.bfloat16)


def on_device(voltages, input_gains):
    block_count, _, per_dev, sample_count = voltages.shape
    spec_len = SPEC
    fft_len = NFFT
    tap_count = TAPS
    frames = voltages[:, 0].transpose(1, 0, 2).reshape(per_dev, block_count, spec_len, fft_len)
    tail_frames = frames[:, :, spec_len - (tap_count - 1) :, :]
    received = from_behind(tail_frames, "tblk", 1)
    shifted = jnp.concatenate([jnp.zeros_like(received[:, :1]), received[:, :-1]], axis=1)
    earlier = jnp.where(lax.axis_index("tblk") == 0, shifted, received)
    extended = jnp.concatenate([earlier, frames], axis=2)
    coefficients = prototype(tap_count, fft_len)
    filtered_sum = jnp.zeros(frames.shape, jnp.float32)
    for tap_index in range(tap_count):
        filtered_sum = filtered_sum + coefficients[tap_index] * extended[
            :, :, tap_index : tap_index + spec_len
        ].astype(jnp.float32)
    filtered = (filtered_sum * input_gains[:, None, None, None]).astype(jnp.bfloat16)
    time_len = block_count * spec_len
    filtered = filtered.reshape(per_dev, time_len, fft_len)
    time_groups = lax.axis_size("tblk")
    chan_groups = lax.axis_size("chan")
    per_chan = CHANNELS // (time_groups * chan_groups)
    dft_table = make_table(CHANNELS, fft_len).reshape(
        time_groups, chan_groups, per_chan, 2, fft_len
    )
    spectra = lax.dot_general(
        dft_table, filtered, (((4,), (2,)), ((), ())), preferred_element_type=jnp.float32
    )
    spectra = spectra.astype(jnp.bfloat16)
    norm_scale = 1.0 / (time_groups * time_len)
    all_inputs = chan_groups * per_dev
    turned = lax.all_to_all(
        lax.all_to_all(spectra, "tblk", split_axis=0, concat_axis=0, tiled=True),
        "chan",
        split_axis=1,
        concat_axis=1,
        tiled=True,
    )
    results = []
    for item in range(turned.shape[2]):
        piece = turned[:, :, item]
        real_cols = []
        swap_cols = []
        for group in range(time_groups):
            real_slab = piece[group, :, 0].reshape(all_inputs, time_len)
            imag_slab = piece[group, :, 1].reshape(all_inputs, time_len)
            real_cols.append(real_slab)
            real_cols.append(imag_slab)
            swap_cols.append(imag_slab)
            swap_cols.append(-real_slab)
        left_rows = jnp.concatenate(real_cols, axis=1)
        swapped = jnp.concatenate(swap_cols, axis=1)
        results.append(hermitian(left_rows, swapped, norm_scale))
    return jnp.stack(results)


def solution(mesh):
    in_specs = (P(None, "tblk", "chan", None), P("chan"))
    out_specs = P(("tblk", "chan"), None, None, None)
    return jax.shard_map(
        on_device, mesh=mesh, in_specs=in_specs, out_specs=out_specs, check_vma=False
    )
```

profile of v0, /device:TPU:1, one launch (start us, length us, event | category | flops | bytes accessed | tf_op | source)
XLA Modules:
  0.0 150.8 jit_solution(13061674725713392327)
XLA Ops:
  0.0 1.2 slice.81
  1.2 0.0 copy-start.1
  1.2 3.8 %collective-permute-start = (bf16[8,8,3,2048]{3,0,2,1:T(8,128)(2,1)S(1)}, bf16[8,8,3,2048]{3,0,2,1:T(8,128)(2,1)S(1)}, u32[]{:S(2)}, u32[]{:S(2)}) collective-permute-start(bf16[8,8,3,2048]{3,0,2,1:T(8,128)(2,1)S(1)} %slice.81), channel_id=1, source_target_pairs={{128,0},{0,128},{129,1},{1,129},{130,2},{2,130},{131,3},{3,131},{1... | collective-permute-start | bytes 2359304 | tf_op jit(solution)/shard_map/ppermute | solution.py:17
  5.0 0.8 multiply_reduce_fusion
  6.5 0.2 broadcast_divide_fusion
  6.7 0.0 copy-start
  6.7 18.4 %multiply_convert_fusion.2 = (bf16[2,128,2,1,2048]{4,1,3,2,0:T(8,128)(2,1)S(1)}, bf16[2,128,2,1,2048]{4,1,3,2,0:T(8,128)(2,1)S(1)}) fusion(s32[2,128,2]{1,2,0:T(2,128)S(1)} %multiply_add_fusion.1), kind=kLoop, calls=%fused_computation.24 | loop fusion | flops 19922944 | bytes 4196352 | tf_op jit(solution)/shard_map/convert
  25.1 0.0 collective-permute-done
  25.1 0.1 pad_select_fusion
  25.2 0.0 copy-done.1
  25.3 0.0 copy-done
  25.3 4.9 %multiply_convert_fusion = bf16[8,8,16,2048]{3,0,2,1:T(8,128)(2,1)S(1)} fusion(bf16[8,8,16,2048]{3,0,2,1:T(8,128)(2,1)S(1)} %bitcast.55, bf16[8,8,3,2048]{3,0,2,1:T(8,128)(2,1)S(1)} %pad_select_fusion, f32[8]{0:T(128)S(1)} %copy-done.1, f32[2048]{0:T(1024)S(1)} %get-tuple-element.20, f32[2048]{0:T(1024)S(1)} %get-tuple-element.21, ...), kind=kLoop, calls=%fused_computation.5 | loop fusion | flops 33554432 | bytes 9207840 | tf_op jit(solution)/shard_map/convert_element_type | solution.py:69
  30.2 2.3 %copy.13 = bf16[8,8,16,2048]{3,2,1,0:T(8,128)(2,1)S(1)} copy(bf16[8,8,16,2048]{3,0,2,1:T(8,128)(2,1)S(1)} %multiply_convert_fusion) | data formatting | bytes 8388608 | tf_op jit(solution)/shard_map/convert_element_type | solution.py:69
  32.5 4.8 %fusion.13 = bf16[2,128,2,2,8,128]{5,1,4,3,2,0:T(8,128)(2,1)S(1)} fusion(bf16[8,128,2048,1,1,1]{2,1,0,5,4,3:T(8,128)(2,1)S(1)} %bitcast.56, bf16[2,128,2,1,2048]{4,1,3,2,0:T(8,128)(2,1)S(1)} %get-tuple-element.24, bf16[2,128,2,1,2048]{4,1,3,2,0:T(8,128)(2,1)S(1)} %get-tuple-element.23), kind=kOutput, calls=%fused_computation.32 | convolution fusion | flops 4304404480 | bytes 10485760 | tf_op jit(solution)/shard_map/dot_general | solution.py:78
  37.2 27.4 %all_to_all.10 = bf16[2,128,2,2,8,128]{5,1,4,3,2,0:T(8,128)(2,1)S(1)} all-to-all(bf16[2,128,2,2,8,128]{5,1,4,3,2,0:T(8,128)(2,1)S(1)} %fusion.13), channel_id=1, replica_groups=mesh['tblk'=2,'chan'=128] {'tblk'}, dimensions={0} | all-to-all | bytes 4194304 | tf_op jit(solution)/shard_map/all_to_all | solution.py:85
  64.6 1.4 copy.14
  66.0 68.5 %all_to_all.11 = bf16[2,128,2,2,8,128]{5,4,3,2,0,1:T(8,128)(2,1)S(1)} all-to-all(bf16[2,128,2,2,8,128]{5,4,3,2,0,1:T(8,128)(2,1)S(1)} %copy.14), channel_id=1, replica_groups=mesh['tblk'=2,'chan'=128] {'chan'}, dimensions={1} | all-to-all | bytes 4194304 | tf_op jit(solution)/shard_map/all_to_all | solution.py:84
  134.4 0.4 fusion.50
  134.8 0.4 copy_bitcast_fusion
  135.2 0.1 fusion.48
  135.3 0.1 slice_bitcast_fusion.3
  135.4 0.1 fusion.46
  135.4 0.1 slice_bitcast_fusion.7
  135.5 1.3 convolution_bitcast_fusion.3
  136.8 1.3 convolution_bitcast_fusion.2
  138.1 1.2 fusion
  139.3 1.3 convolution_bitcast_fusion.1
  140.6 1.3 convolution_bitcast_fusion
  141.9 2.5 %fusion.1 = bf16[1,2,1024,1024]{3,2,1,0:T(8,128)(2,1)} fusion(f32[1,1,1024,1024]{3,2,1,0:T(8,128)S(1)} %convolution_bitcast_fusion, f32[1,1,1024,1024]{3,2,1,0:T(8,128)S(1)} %convolution_bitcast_fusion.1), kind=kLoop, calls=%fused_computation.3 | loop fusion | flops 6291456 | bytes 12582912 | tf_op jit(solution)/shard_map/convert_element_type | solution.py:49
  144.4 6.3 %pad_maximum_fusion = bf16[2,2,1024,1024]{3,2,1,0:T(8,128)(2,1)} fusion(bf16[1,2,1024,1024]{3,2,1,0:T(8,128)(2,1)} %fusion.1, bf16[1,2,1024,1024]{3,2,1,0:T(8,128)(2,1)S(1)} %fusion), kind=kLoop, calls=%fused_computation.4 | loop fusion | flops 4194304 | bytes 16777216 | tf_op jit(solution)/shard_map/stack | solution.py:106
  (3 shorter events, 0.1 us)
Async XLA Ops:
  1.2 24.1 %copy-start.1 = (f32[8]{0:T(128)S(1)}, f32[8]{0:T(128)}, u32[]{:S(2)}) copy-start(f32[8]{0:T(128)} %param.3) | copy-start | bytes 100
  1.2 23.9 %collective-permute-start = (bf16[8,8,3,2048]{3,0,2,1:T(8,128)(2,1)S(1)}, bf16[8,8,3,2048]{3,0,2,1:T(8,128)(2,1)S(1)}, u32[]{:S(2)}, u32[]{:S(2)}) collective-permute-start(bf16[8,8,3,2048]{3,0,2,1:T(8,128)(2,1)S(1)} %slice.81), channel_id=1, source_target_pairs={{128,0},{0,128},{129,1},{1,129},{130,2},{2,130},{131,3},{3,131},{1... | collective-permute-start | bytes 2359304 | tf_op jit(solution)/shard_map/ppermute | solution.py:17
  6.7 18.6 %copy-start = (bf16[8,1,8,32768]{3,2,1,0:T(8,128)(2,1)S(1)}, bf16[8,1,8,32768]{3,2,1,0:T(8,128)(2,1)}, u32[]{:S(2)}) copy-start(bf16[8,1,8,32768]{3,2,1,0:T(8,128)(2,1)} %param.2) | copy-start | bytes 12582916
where the time goes:
time: 151 us
  blocking collectives  95.8 us (63%)
  other arithmetic  34.5 us (23%)
  matrix products  9.91 us (7%)
  local copies, waits for them, and re-layouts  5.78 us (4%)
  starting transfers between devices  3.83 us (3%)
    all_to_all x1, blocking collectives, on_device(): lax.all_to_all(lax.all_to_all(spectra, 'tblk', split_axis=0, concat_axis=...  68.5 us
    all_to_all x1, blocking collectives, on_device(): lax.all_to_all(spectra, 'tblk', split_axis=0, concat_axis=0, tiled=True)  27.4 us
    another operation x1, other arithmetic  18.4 us
    another operation x1, other arithmetic, on_device(): return jnp.stack(results)  6.35 us
    dot_general x4, matrix products, products(): lax.dot_general(left_side, right_side, (((1,), (1,)), ((), ())), preferre...  5.13 us
    convert_element_type x1, other arithmetic, on_device(): (filtered_sum * input_gains[:, None, None, None]).astype(jnp.bfloat16)  4.88 us
    dot_general x1, matrix products, on_device(): lax.dot_general(dft_table, filtered, (((4,), (2,)), ((), ())), preferred_...  4.78 us
    ppermute x1, starting transfers between devices, from_behind(): return lax.ppermute(block, axis, route)  3.83 us
  transfers between devices with their start and end apart: 1, of which 0 were waited for; matrix products, arithmetic and copies ran while one was open for 13% of the time, Pallas kernels for 0%

commit v1 on v0

v1 whole, which is shorter than its diff:
```python
import functools
import math

import jax
import jax.numpy as jnp
import numpy as np
from jax import lax
from jax.experimental import pallas as pl
from jax.experimental.pallas import tpu as pltpu
from jax.sharding import PartitionSpec as P

CHANNELS = 512
NFFT = 2048
HALF = NFFT // 2
TAPS = 4
SPEC = 16
BLKS = 8
LANES = 128
SUB = 8
VMEM_LIMIT = 56 * 1024 * 1024


def prototype():
    positions = np.arange(TAPS * NFFT, dtype=np.float64) + 0.5
    window = 0.5 - 0.5 * np.cos(2.0 * math.pi * positions / (TAPS * NFFT))
    shape_fn = np.sinc(positions / NFFT - TAPS / 2.0) * window
    shape_fn = shape_fn / np.sqrt(TAPS * np.mean(shape_fn * shape_fn))
    return shape_fn.reshape(TAPS, NFFT).astype(np.float32)


def half_tables():
    chan = np.arange(CHANNELS, dtype=np.int64)
    sample = np.arange(HALF, dtype=np.int64)
    angle = (chan[:, None] * sample[None, :] % NFFT) * (2.0 * math.pi / NFFT)
    norm = 1.0 / math.sqrt(NFFT)
    real, imag = np.cos(angle) * norm, -np.sin(angle) * norm
    table = np.stack(
        [np.concatenate([real[r::2], imag[r::2]], axis=0) for r in range(2)]
    )
    return table.astype(jnp.bfloat16)


def filter_bank(place_ref, v_ref, gain_ref, coef_ref, table_ref, out_ref, frames, extra, rows, tiles):
    group = pl.program_id(0)
    first = 16 * group
    gain = gain_ref[...]
    slot = pl.multiple_of(first + SUB * place_ref[0], SUB)

    @pl.when(group == 0)
    def _():
        extra[...] = jnp.zeros_like(extra)

    def columns(j, carry):
        low = pl.multiple_of(j * LANES, LANES)
        weights = [
            [coef_ref[k : k + 1, pl.ds(low + h * HALF, LANES)] * gain for k in range(TAPS)]
            for h in range(2)
        ]
        window = [[None] * TAPS for _ in range(2)]
        for s in range(SPEC + TAPS - 1):
            sums = []
            for h in range(2):
                if s < SPEC:
                    now = v_ref[:, pl.ds(low + s * NFFT + h * HALF, LANES)].astype(jnp.float32)
                else:
                    now = None
                window[h] = window[h][1:] + [now]
                total = None
                for k in range(TAPS):
                    if window[h][k] is not None:
                        term = window[h][k] * weights[h][k]
                        total = term if total is None else total + term
                sums.append(total)
            pair = (sums[0] + sums[1], sums[0] - sums[1])
            for half in range(2):
                if s < SPEC:
                    frames[half, j, pl.ds(pl.multiple_of(s * 64 + first, 16), 16), :] = pair[half]
                else:
                    extra[half, j, pl.ds(pl.multiple_of((s - SPEC) * 80 + slot, SUB), 16), :] = pair[half]
        return carry

    lax.fori_loop(0, HALF // LANES, columns, 0)

    @pl.when(group == pl.num_programs(0) - 1)
    def _():
        lane = lax.broadcasted_iota(jnp.int32, (1, LANES), 1)
        dest = out_ref.shape[0]
        for part in range(2):
            base = 512 - 512 * part
            for half in range(2):
                for i in range(SUB):
                    for j in range(HALF // LANES):
                        picked = frames[half, j, pl.ds(base + i, 64, stride=SUB), :]
                        rows[i * 64 : (i + 1) * 64, j * LANES : (j + 1) * LANES] = picked.astype(jnp.bfloat16)
                spectra = lax.dot_general(
                    table_ref[half], rows[...], (((1,), (1,)), ((), ())),
                    preferred_element_type=jnp.float32,
                )
                for pair in range(SUB // 2):
                    real = spectra[:dest, pair * LANES : (pair + 1) * LANES]
                    imag = spectra[dest:, pair * LANES : (pair + 1) * LANES]
                    tiles[pl.ds(2 * pair, dest, stride=SUB), :] = jnp.where(
                        lane < 64, real, pltpu.roll(imag, 64, 1)
                    )
                    tiles[pl.ds(2 * pair + 1, dest, stride=SUB), :] = jnp.where(
                        lane < 64, pltpu.roll(real, 64, 1), imag
                    )
                out_ref[:, 2 * part + half] = tiles[...].reshape(dest, SUB, LANES).astype(jnp.bfloat16)
        parts = []
        for half in range(2):
            rows[...] = jnp.zeros_like(rows)
            for i in range(SUB):
                for j in range(HALF // LANES):
                    picked = jnp.concatenate(
                        [extra[half, j, pl.ds(80 * s + i, 8, stride=SUB), :] for s in range(TAPS - 1)]
                        + [jnp.zeros((8, LANES), jnp.float32)],
                        axis=0,
                    )
                    rows[i * 32 : (i + 1) * 32, j * LANES : (j + 1) * LANES] = picked.astype(jnp.bfloat16)
            spectra = lax.dot_general(
                table_ref[half], rows[:256], (((1,), (1,)), ((), ())),
                preferred_element_type=jnp.float32,
            )
            parts += [spectra[:dest], spectra[dest:]]
        for i in range(SUB):
            merged = None
            for slot_index in range(4):
                piece = parts[slot_index][:, (i // 4) * LANES : (i // 4 + 1) * LANES]
                shift = (32 * slot_index - 32 * (i % 4)) % LANES
                if shift:
                    piece = pltpu.roll(piece, shift, 1)
                merged = piece if merged is None else jnp.where(lane < 32 * slot_index, merged, piece)
            tiles[pl.ds(i, dest, stride=SUB), :] = merged
        out_ref[:, 4] = tiles[...].reshape(dest, SUB, LANES).astype(jnp.bfloat16)


def correlate(scale, recv_ref, out_ref, left, swap):
    item = pl.program_id(0)
    block = pl.program_id(1)
    count = left.shape[0]
    half = recv_ref.shape[0] // 2

    @pl.when(block == 0)
    def _():
        lane = lax.broadcasted_iota(jnp.int32, (1, LANES), 1)

        def put(column, piece):
            left[:, column * LANES : (column + 1) * LANES] = piece.astype(jnp.bfloat16)
            turned = pltpu.roll(piece, 64, 1)
            swap[:, column * LANES : (column + 1) * LANES] = jnp.where(lane < 64, turned, -turned).astype(jnp.bfloat16)

        def take(t, tile):
            return recv_ref[t * half : (t + 1) * half, tile].astype(jnp.float32).reshape(count, LANES)

        for t in range(2):
            put(2 * t, take(t, item))
            first = take(t, 2 + item)
            other = take(1 - t, 4)
            other = jnp.where(item == 0, other, pltpu.roll(other, 64, 1))
            other = jnp.where(
                lane < 32, other, jnp.where((lane >= 64) & (lane < 96), pltpu.roll(other, 32, 1), 0.0)
            )
            put(2 * t + 1, first + other)

    rows = out_ref.shape[2]
    at = pl.ds(pl.multiple_of(block * rows, rows), rows)
    for kind, source in enumerate((left, swap)):
        product = lax.dot_general(
            source[at, :], left[...], (((1,), (1,)), ((), ())), preferred_element_type=jnp.float32
        )
        out_ref[0, kind] = (product * scale).astype(jnp.bfloat16)


def on_device(voltages, input_gains):
    per_dev = voltages.shape[2]
    samples = voltages.shape[3]
    groups = lax.axis_size("tblk") * lax.axis_size("chan")
    inputs = lax.axis_size("chan") * per_dev
    coefs = jnp.asarray(prototype())
    table = jnp.asarray(half_tables())
    place = lax.axis_index("tblk").astype(jnp.int32).reshape(1)
    gain_rows = jnp.broadcast_to(jnp.tile(input_gains, 2)[:, None], (16, LANES))
    sent = pl.pallas_call(
        filter_bank,
        grid=(BLKS // 2,),
        in_specs=[
            pl.BlockSpec(memory_space=pltpu.SMEM),
            pl.BlockSpec((16, samples), lambda g: (g, 0)),
            pl.BlockSpec((16, LANES), lambda g: (0, 0)),
            pl.BlockSpec((TAPS, NFFT), lambda g: (0, 0)),
            pl.BlockSpec((2, CHANNELS, HALF), lambda g: (0, 0, 0)),
        ],
        out_specs=pl.BlockSpec((groups, 5, SUB, LANES), lambda g: (0, 0, 0, 0)),
        out_shape=jax.ShapeDtypeStruct((groups, 5, SUB, LANES), jnp.bfloat16),
        scratch_shapes=[
            pltpu.VMEM((2, HALF // LANES, SPEC * 64, LANES), jnp.float32),
            pltpu.VMEM((2, HALF // LANES, (TAPS - 1) * 80, LANES), jnp.float32),
            pltpu.VMEM((512, HALF), jnp.bfloat16),
            pltpu.VMEM((groups * SUB, LANES), jnp.float32),
        ],
        compiler_params=pltpu.CompilerParams(vmem_limit_bytes=VMEM_LIMIT),
        name="filter_bank",
    )(place, voltages.reshape(BLKS * per_dev, samples), gain_rows, coefs, table)
    turned = lax.all_to_all(sent, ("tblk", "chan"), split_axis=0, concat_axis=0, tiled=True)
    scale = 1.0 / (BLKS * SPEC * lax.axis_size("tblk"))
    items = CHANNELS // groups
    block = 256
    return pl.pallas_call(
        functools.partial(correlate, scale),
        grid=(items, inputs // block),
        in_specs=[pl.BlockSpec((groups, 5, SUB, LANES), lambda m, r: (0, 0, 0, 0))],
        out_specs=pl.BlockSpec((1, 2, block, inputs), lambda m, r: (m, 0, r, 0)),
        out_shape=jax.ShapeDtypeStruct((items, 2, inputs, inputs), jnp.bfloat16),
        scratch_shapes=[
            pltpu.VMEM((inputs, 4 * LANES), jnp.bfloat16),
            pltpu.VMEM((inputs, 4 * LANES), jnp.bfloat16),
        ],
        compiler_params=pltpu.CompilerParams(vmem_limit_bytes=VMEM_LIMIT),
        name="correlate",
    )(turned)


def solution(mesh):
    in_specs = (P(None, "tblk", "chan", None), P("chan"))
    out_specs = P(("tblk", "chan"), None, None, None)
    return jax.shard_map(
        on_device, mesh=mesh, in_specs=in_specs, out_specs=out_specs, check_vma=False
    )
```

time: 151 us -> 105 us (0.70)
  other arithmetic: 34.5 us -> 0 us
  Pallas kernels: 0 us -> 23.3 us
  blocking collectives: 95.8 us -> 80.3 us
  matrix products: 9.91 us -> 0 us
  local copies, waits for them, and re-layouts: 5.78 us -> 1.41 us
  starting transfers between devices: 3.83 us -> 0 us
    another operation x2 -> x0, other arithmetic: 24.7 us -> none
    pallas_call x0 -> x2, Pallas kernels: none -> 23.3 us  [the longest x1 12.4 us: on_device(): pl.pallas_call(filter_bank, grid=(BLKS // 2,), in_specs=[pl.BlockSpec(mem...]
    all_to_all x2 -> x1, blocking collectives: 95.8 us -> 80.3 us  [on_device(): lax.all_to_all(sent, ('tblk', 'chan'), split_axis=0, concat_axis=0, tiled...]
    dot_general x5 -> x0, matrix products: 9.91 us -> none  [the longest x4 5.13 us: products(): lax.dot_general(left_side, right_side, (((1,), (1,)), ((), ())), preferre...]
    convert_element_type x3 -> x0, other arithmetic: 8.63 us -> none  [the longest x1 4.88 us: on_device(): (filtered_sum * input_gains[:, None, None, None]).astype(jnp.bfloat16)]
    ppermute x1 -> x0, starting transfers between devices: 3.83 us -> none  [from_behind(): return lax.ppermute(block, axis, route)]
    convert_element_type x1 -> x0, local copies, waits for them, and re-layouts: 2.3 us -> none  [on_device(): (filtered_sum * input_gains[:, None, None, None]).astype(jnp.bfloat16)]
    slice x4 -> x0, local copies, waits for them, and re-layouts: 1.61 us -> none  [the longest x1 1.18 us: on_device(): tail_frames = frames[:, :, spec_len - (tap_count - 1):, :]]
  transfers between devices with their start and end apart: 1 -> 0, of which waited for: 0 -> 0; matrix products, arithmetic and copies ran while one was open for 13% -> 0% of each run, Pallas kernels for 0% -> 0%
where the time goes in v1:
time: 105 us
  blocking collectives  80.3 us (76%)
  Pallas kernels  23.3 us (22%)
  local copies, waits for them, and re-layouts  1.41 us (1%)
    all_to_all x1, blocking collectives, on_device(): lax.all_to_all(sent, ('tblk', 'chan'), split_axis=0, concat_axis=0, tiled...  80.3 us
    pallas_call x1, Pallas kernels, on_device(): pl.pallas_call(filter_bank, grid=(BLKS // 2,), in_specs=[pl.BlockSpec(mem...  12.4 us
    pallas_call x1, Pallas kernels, on_device(): pl.pallas_call(functools.partial(correlate, scale), grid=(items, inputs /...  10.9 us

profile of v1, /device:TPU:1, one launch (start us, length us, event | category | flops | bytes accessed | tf_op | source)
XLA Modules:
  0.0 105.1 jit_solution(15298120978963196042)
XLA Ops:
  0.0 0.7 tile.2
  0.7 0.1 broadcast_in_dim.7
  0.7 0.7 broadcast_in_dim.8.gain_ref
  1.4 12.4 %filter_bank.1 = bf16[256,5,8,128]{3,2,1,0:T(8,128)(2,1)} custom-call(s32[1]{0:T(128)} %bitcast.place_ref, bf16[64,32768]{1,0:T(8,128)(2,1)} %bitcast.2, f32[16,128]{1,0:T(8,128)} %broadcast_in_dim.8.gain_ref, f32[4,2048]{1,0:T(4,128)} %constant.10.clone.coef_ref, bf16[2,512,1024]{2,1,0:T(8,128)(2,1)} %constant.11.clone.table_ref), custom_call_target="tpu_custom_call" | custom-call | tf_op jit(solution)/shard_map/filter_bank/pallas_call | solution.py:183
  13.8 80.3 %all_to_all.5.recv_ref = bf16[256,5,8,128]{3,2,1,0:T(8,128)(2,1)} all-to-all(bf16[256,5,8,128]{3,2,1,0:T(8,128)(2,1)} %filter_bank.1), channel_id=1, replica_groups=mesh['tblk'=2,'chan'=128] {'tblk','chan'}, dimensions={0} | all-to-all | bytes 5242880 | tf_op jit(solution)/shard_map/all_to_all | solution.py:204
  94.1 10.9 %correlate.1 = bf16[2,2,1024,1024]{3,2,1,0:T(8,128)(2,1)} custom-call(bf16[256,5,8,128]{3,2,1,0:T(8,128)(2,1)} %all_to_all.5.recv_ref), custom_call_target="tpu_custom_call" | custom-call | tf_op jit(solution)/shard_map/correlate/pallas_call | solution.py:208

commit v2 on v0

v2 whole, which is shorter than its diff:
```python
import functools
import math

import jax
import jax.numpy as jnp
import numpy as np
from jax import lax
from jax.experimental import pallas as pl
from jax.experimental.pallas import tpu as pltpu
from jax.sharding import Mesh, PartitionSpec as P

CHANNELS = 512
NFFT = 2048
HALF = NFFT // 2
TAPS = 4
SPEC = 16
BLKS = 8
LANES = 128
SUB = 8
RING = 8
AXES = ("yh", "yl", "z", "x", "c")
DEVICES = 256
FLAT = 32
MIB = 1024 * 1024
BF16 = jnp.bfloat16
F32 = jnp.float32


def prototype():
    positions = np.arange(TAPS * NFFT, dtype=np.float64) + 0.5
    window = 0.5 - 0.5 * np.cos(2.0 * math.pi * positions / (TAPS * NFFT))
    shape_fn = np.sinc(positions / NFFT - TAPS / 2.0) * window
    shape_fn = shape_fn / np.sqrt(TAPS * np.mean(shape_fn * shape_fn))
    return shape_fn.reshape(TAPS, NFFT).astype(np.float32)


def quarter_tables():
    owner = np.arange(DEVICES, dtype=np.int64).reshape(4, RING, 8).swapaxes(0, 1).reshape(DEVICES)
    sample = np.arange(HALF, dtype=np.int64)
    norm = 1.0 / math.sqrt(NFFT)
    quarters = []
    for r in range(2):
        angle = ((2 * owner[:, None] + r) * sample % NFFT) * (2.0 * math.pi / NFFT)
        quarters += [np.cos(angle) * norm, -np.sin(angle) * norm]
    return np.stack(quarters).astype(BF16)


def row_gain(gain_ref):
    row = lax.broadcasted_iota(jnp.int32, (2 * SUB, LANES), 0) % SUB
    gain = jnp.zeros((2 * SUB, LANES), F32)
    for i in range(SUB):
        gain = jnp.where(row == i, gain_ref[i], gain)
    return gain


def filter_frames(load, gain_ref, coef_ref, outputs, emit):
    gain = row_gain(gain_ref)

    def columns(j, carry):
        low = pl.multiple_of(j * LANES, LANES)
        weights = [
            [coef_ref[k : k + 1, pl.ds(low + h * HALF, LANES)] * gain for k in range(TAPS)]
            for h in range(2)
        ]
        held = {}
        for s in outputs:
            sums = []
            for h in range(2):
                total = None
                for k in range(TAPS):
                    frame = s - (TAPS - 1) + k
                    if frame < 0 or frame >= SPEC:
                        continue
                    if (frame, h) not in held:
                        held[frame, h] = load(frame, low + h * HALF).astype(F32)
                    term = held[frame, h] * weights[h][k]
                    total = term if total is None else total + term
                sums.append(total)
            emit(s, j, sums[0] + sums[1], sums[0] - sums[1])
        return carry

    lax.fori_loop(0, HALF // LANES, columns, 0)


def place_rows(rows, half, group, i, j, picked):
    packed = picked.astype(BF16)
    for q in (2 * half, 2 * half + 1):
        at = group * 256 + (i // 4) * LANES + ((i + q) % 4) * 32
        rows[q, at : at + 32, j * LANES : (j + 1) * LANES] = packed


def transform(table, half, rows, spec):
    for q in (2 * half, 2 * half + 1):
        spec[q] = lax.dot_general(
            table[q], rows[q], (((1,), (1,)), ((), ())), preferred_element_type=F32
        )


def owner_tiles(spec, tiles, group, turn, start, count):
    lane = lax.broadcasted_iota(jnp.int32, (1, LANES), 1)
    for i in range(SUB):
        p = i % 4
        at = group * 256 + (i // 4) * LANES
        merged = None
        for r in range(4):
            piece = spec[(r - p) % 4, pl.ds(start, count), at : at + LANES]
            merged = piece if merged is None else jnp.where(lane < 32 * r, merged, piece)
        if (turn - p) % 4:
            merged = pltpu.roll(merged, 32 * ((turn - p) % 4), 1)
        tiles[pl.ds(i, count, stride=SUB), :] = merged


def last_frames(y_ref, z_ref, c_ref, gain_ref, high_ref, mid_ref, coef_ref, table_ref,
                own_ref, other_ref, far_ref, near_ref, tail_ref, frames, extra, rows, spec, tiles, held, sem):
    step = pl.program_id(0)
    slot_row = pl.multiple_of(16 * step + SUB * (y_ref[0] >> 1), SUB)
    fetch = pltpu.make_async_copy(table_ref, held, sem)

    @pl.when(step == 0)
    def _():
        fetch.start()
        extra[...] = jnp.zeros_like(extra)

    def load(frame, low):
        if frame >= 12:
            return high_ref[:, pl.ds(low + (frame - 12) * NFFT, LANES)]
        return mid_ref[:, pl.ds(low + (frame - 8) * NFFT, LANES)]

    def emit(s, j, total, diff):
        if s < SPEC:
            at = pl.ds(pl.multiple_of((s - 12) * 64 + 16 * step, 16), 16)
            frames[0, j, at, :] = total
            frames[1, j, at, :] = diff
        else:
            at = pl.ds(pl.multiple_of((s - SPEC) * 80 + slot_row, SUB), 16)
            extra[0, j, at, :] = total
            extra[1, j, at, :] = diff

    filter_frames(load, gain_ref, coef_ref, range(12, SPEC + TAPS - 1), emit)

    @pl.when(step == pl.num_programs(0) - 1)
    def _():
        for half in range(2):
            for i in range(SUB):
                for j in range(HALF // LANES):
                    place_rows(rows, half, 0, i, j, frames[half, j, pl.ds(i, 32, stride=SUB), :])
                    picked = jnp.concatenate(
                        [extra[half, j, pl.ds(80 * s + i, 8, stride=SUB), :] for s in range(TAPS - 1)]
                        + [jnp.zeros((8, LANES), F32)],
                        axis=0,
                    )
                    place_rows(rows, half, 1, i, j, picked)
            if half == 0:
                fetch.wait()
            transform(held, half, rows, spec)
        core = c_ref[0]
        sign = 1 - 2 * core
        for slot, away in enumerate((1, 2, 3, -1, -2, -3, 4, 0)):
            zdest = (z_ref[0] + (sign * away if slot < 6 else away) + RING) & (RING - 1)
            tile = tiles.at[slot]
            owner_tiles(spec, tile, 0, 3, pl.multiple_of(zdest * FLAT, FLAT), FLAT)
            parts = tile[...].reshape(FLAT // 2, 2, SUB, LANES).astype(BF16)
            if slot < 3:
                for owner_core in range(2):
                    own_ref[slot, owner_core] = parts[:, owner_core]
            elif slot < 6:
                for owner_core in range(2):
                    other_ref[slot - 3, owner_core] = parts[:, owner_core]
            else:
                kept_ref = far_ref if slot == 6 else near_ref
                for owner_core in range(2):
                    @pl.when(core == owner_core)
                    def _(owner_core=owner_core):
                        kept_ref[...] = parts[:, owner_core]
                        other_ref[3, slot - 6] = parts[:, 1 - owner_core]
        store_owners(spec, tiles, 8, 1, 0, tail_ref)


def store_owners(spec, tiles, first, group, turn, out_ref):
    for z in range(RING):
        tile = tiles.at[first + z]
        owner_tiles(spec, tile, group, turn, z * FLAT, FLAT)
        out_ref[:, z] = tile[...].reshape(4, SUB, SUB, LANES).astype(BF16)


def main_frames(gain_ref, low_ref, mid_ref, coef_ref, table_ref, out_ref, frames, rows, spec, tiles, held, sem):
    step = pl.program_id(0)
    fetch = pltpu.make_async_copy(table_ref, held, sem)
    pl.when(step == 0)(fetch.start)

    def load(frame, low):
        if frame < 8:
            return low_ref[:, pl.ds(low + frame * NFFT, LANES)]
        return mid_ref[:, pl.ds(low + (frame - 8) * NFFT, LANES)]

    def emit(s, j, total, diff):
        at = pl.ds(pl.multiple_of(s * 64 + 16 * step, 16), 16)
        frames[0, j, at, :] = total
        frames[1, j, at, :] = diff

    filter_frames(load, gain_ref, coef_ref, range(12), emit)

    @pl.when(step == pl.num_programs(0) - 1)
    def _():
        for half in range(2):
            for group in range(3):
                for i in range(SUB):
                    for j in range(HALF // LANES):
                        picked = frames[half, j, pl.ds(group * 256 + i, 32, stride=SUB), :]
                        place_rows(rows, half, group, i, j, picked)
            if half == 0:
                fetch.wait()
            transform(held, half, rows, spec)
        for group in range(3):
            store_owners(spec, tiles, RING * group, group, group, out_ref.at[group])


def complete(main_ref, tail_ref, out_ref):
    first = main_ref[0].astype(F32) + tail_ref[...].astype(F32)
    out_ref[:, 0] = first.astype(BF16)
    for group in range(1, 3):
        out_ref[:, group] = main_ref[group]


def sort_y(y_ref, c_ref, one_ref, two_ref, three_ref, part_ref, far_ref, near_ref, next_ref,
           out0_ref, out1_ref, out2_ref, out3_ref):
    core = c_ref[0]
    for dy, out_ref in enumerate((out0_ref, out1_ref, out2_ref, out3_ref)):
        at = pl.ds(((y_ref[0] + dy) & 3) * 4, 4)
        for j, ref in enumerate((one_ref, two_ref, three_ref)):
            for r in range(2):
                out_ref[2 * j + r] = ref[core, r, at]
                out_ref[6 + 2 * j + r] = part_ref[j, r, at]
        for r in range(2):
            out_ref[12 + r] = far_ref[r, at]
        out_ref[14] = near_ref[at]
        out_ref[15] = next_ref[at]


def sort_x(x_ref, a0_ref, a1_ref, a2_ref, a3_ref, out0_ref, out1_ref, out2_ref, out3_ref):
    for dx, out_ref in enumerate((out0_ref, out1_ref, out2_ref, out3_ref)):
        owner_x = (x_ref[0] + dx) & 3
        for dy, ref in enumerate((a0_ref, a1_ref, a2_ref, a3_ref)):
            out_ref[dy] = ref[:, owner_x]


def arrange(y_ref, z_ref, x_ref, c_ref, a0_ref, a1_ref, a2_ref, a3_ref, out_ref):
    y, z, x, core = y_ref[0], z_ref[0], x_ref[0], c_ref[0]
    sign = 1 - 2 * core
    origin = []
    for j in range(3):
        origin += [(-sign * (j + 1), core), (-sign * (j + 1), 1 - core)]
    for j in range(3):
        origin += [(sign * (j + 1), 1 - core), (sign * (j + 1), core)]
    origin += [(4, core), (4, 1 - core), (0, core), (0, 1 - core)]
    for dx, ref in enumerate((a0_ref, a1_ref, a2_ref, a3_ref)):
        xsrc = (x - dx + 4) & 3
        for dy in range(4):
            ysrc = (y - dy + 4) & 3
            for k, (away, source_core) in enumerate(origin):
                zsrc = (z + away + RING) & (RING - 1)
                out_ref[((ysrc * RING + zsrc) * 4 + xsrc) * 2 + source_core] = ref[dy, k]


def correlate(scale, main_ref, last_ref, out_ref, left, swap):
    item = pl.program_id(0)
    block = pl.program_id(1)
    half = DEVICES // 2

    def collect(which):
        lane = lax.broadcasted_iota(jnp.int32, (1, LANES), 1)
        rows = left.shape[0]
        for t in range(2):
            here = slice(t * half, (t + 1) * half)
            groups = [main_ref[here, g] for g in range(3)] + [last_ref[here]]
            groups = [g.astype(F32).reshape(rows, LANES) for g in groups]

            def quarter(q):
                merged = None
                for r in range(4):
                    piece = groups[(r - q) % 4]
                    merged = piece if merged is None else jnp.where(lane < 32 * r, merged, piece)
                return merged

            real = quarter(2 * which)
            imag = pltpu.roll(quarter(2 * which + 1), LANES - 32, 1)
            first = slice(2 * t * LANES, (2 * t + 1) * LANES)
            second = slice((2 * t + 1) * LANES, (2 * t + 2) * LANES)
            left[:, first] = real.astype(BF16)
            swap[:, second] = (-real).astype(BF16)
            imag = imag.astype(BF16)
            left[:, second] = imag
            swap[:, first] = imag

    for which in range(2):
        pl.when((block == 0) & (item == which))(functools.partial(collect, which))

    count = out_ref.shape[2]
    at = pl.ds(pl.multiple_of(block * count, count), count)
    for kind, source in enumerate((left, swap)):
        product = lax.dot_general(
            source[at, :], left[...], (((1,), (1,)), ((), ())), preferred_element_type=F32
        )
        out_ref[0, kind] = (product * scale).astype(BF16)


def along_ring(block, distance):
    route = []
    for z in range(RING):
        for c in range(2):
            target = (z + (distance if c == 0 else -distance)) % RING
            route.append((z * 2 + c, target * 2 + c))
    return lax.ppermute(block, ("z", "c"), route)


def along(block, axis, distance, size):
    return lax.ppermute(block, axis, [(i, (i + distance) % size) for i in range(size)])


def call(kernel, grid, in_specs, out_specs, out_shape, scratch, name, limit):
    return pl.pallas_call(
        kernel, grid=grid, in_specs=in_specs, out_specs=out_specs, out_shape=out_shape,
        scratch_shapes=scratch, name=name,
        compiler_params=pltpu.CompilerParams(vmem_limit_bytes=limit * MIB),
    )


def whole(*shape):
    return pl.BlockSpec(shape, lambda *ids: (0,) * len(shape))


SMEM = pl.BlockSpec(memory_space=pltpu.SMEM)


def simple(kernel, scalars, arrays, shapes, name):
    return call(
        kernel, (1,), [SMEM] * len(scalars) + [whole(*a.shape) for a in arrays],
        [whole(*s) for s in shapes], [jax.ShapeDtypeStruct(s, BF16) for s in shapes], [], name, 8,
    )(*scalars, *arrays)


def on_device(voltages, input_gains):
    per_dev = voltages.shape[2]
    samples = voltages.shape[3]
    inputs = 128 * per_dev
    coefs = jnp.asarray(prototype())
    table = jnp.asarray(quarter_tables())
    y, z, x, core = [
        lax.axis_index(a).astype(jnp.int32).reshape(1) for a in (("yh", "yl"), "z", "x", "c")
    ]
    stream = voltages.reshape(BLKS * per_dev, samples)
    quarter = samples // 4
    tile = (SUB, LANES)
    tables = [whole(TAPS, NFFT), pl.BlockSpec(memory_space=pl.ANY)]
    table_scratch = [pltpu.VMEM((4, DEVICES, HALF), BF16), pltpu.SemaphoreType.DMA]

    slab = (FLAT // 2,) + tile
    owners = (4, RING, SUB) + tile
    last_shapes = [(3, 2) + slab, (4, 2) + slab, slab, slab, owners]
    own, other, far, near, tail = call(
        last_frames, (BLKS // 2,),
        [
            SMEM, SMEM, SMEM, SMEM,
            pl.BlockSpec((16, quarter), lambda g: (g, 3)),
            pl.BlockSpec((16, quarter), lambda g: (g, 2)),
        ] + tables,
        [whole(*s) for s in last_shapes], [jax.ShapeDtypeStruct(s, BF16) for s in last_shapes],
        [
            pltpu.VMEM((2, HALF // LANES, 256, LANES), F32),
            pltpu.VMEM((2, HALF // LANES, (TAPS - 1) * 80, LANES), F32),
            pltpu.VMEM((4, 512, HALF), BF16),
            pltpu.VMEM((4, DEVICES, 512), F32),
            pltpu.VMEM((16, FLAT * SUB, LANES), F32),
        ] + table_scratch,
        "last_frames", 56,
    )(y, z, core, input_gains, stream, stream, coefs, table)
    tail = along(tail, "yh", 1, 2)
    other = along(other, "c", 1, 2)
    main_gains, other = lax.optimization_barrier((input_gains, other))
    far = along_ring(jnp.stack([far, other[3, 0]]), 4)
    ring = [along_ring(jnp.stack([own[j], other[j]], axis=1), j + 1) for j in range(3)]

    main = call(
        main_frames, (BLKS // 2,),
        [
            SMEM,
            pl.BlockSpec((16, 2 * quarter), lambda g: (g, 0)),
            pl.BlockSpec((16, quarter), lambda g: (g, 2)),
        ] + tables,
        whole(3, *owners), jax.ShapeDtypeStruct((3,) + owners, BF16),
        [
            pltpu.VMEM((2, HALF // LANES, 768, LANES), F32),
            pltpu.VMEM((4, 768, HALF), BF16),
            pltpu.VMEM((4, DEVICES, 768), F32),
            pltpu.VMEM((3 * RING, FLAT * SUB, LANES), F32),
        ] + table_scratch,
        "main_frames", 56,
    )(main_gains, stream, stream, coefs, table)
    ring, far, tail, main = lax.optimization_barrier((ring, far, tail, main))
    packed = (DEVICES, 3) + tile
    main, = simple(
        complete, (), (main.reshape((3, DEVICES) + tile), tail.reshape((DEVICES,) + tile)), [packed], "complete"
    )
    main = lax.all_to_all(main, AXES, split_axis=0, concat_axis=0, tiled=True)

    leaving = jnp.stack([lax.dynamic_index_in_dim(a, 1 - core[0], 0, keepdims=False) for a in ring])
    part = along(leaving, "c", 1, 2)
    by_y = simple(
        sort_y, (y, core), (*ring, part, far, near, other[3, 1]), [(16, 4) + tile] * 4, "sort_y"
    )
    by_y = [by_y[0]] + [along(by_y[d], ("yh", "yl"), d, 4) for d in range(1, 4)]
    by_x = simple(sort_x, (x,), by_y, [(4, 16) + tile] * 4, "sort_x")
    by_x = [by_x[0]] + [along(by_x[d], "x", d, 4) for d in range(1, 4)]
    last, = simple(arrange, (y, z, x, core), by_x, [(DEVICES,) + tile], "arrange")

    scale = 1.0 / (BLKS * SPEC * lax.axis_size("yh"))
    block = 512
    return call(
        functools.partial(correlate, scale), (2, inputs // block),
        [whole(*packed), whole(DEVICES, *tile)],
        pl.BlockSpec((1, 2, block, inputs), lambda m, r: (m, 0, r, 0)),
        jax.ShapeDtypeStruct((2, 2, inputs, inputs), BF16),
        [pltpu.VMEM((inputs, 4 * LANES), BF16), pltpu.VMEM((inputs, 4 * LANES), BF16)],
        "correlate", 28,
    )(main, last)


def solution(mesh):
    fine = Mesh(mesh.devices.reshape(2, 2, RING, 4, 2), AXES)
    inputs = ("yl", "z", "x", "c")
    return jax.shard_map(
        on_device, mesh=fine, in_specs=(P(None, "yh", inputs, None), P(inputs)),
        out_specs=P(AXES, None, None, None), check_vma=False,
    )
```

time: 151 us -> 96.6 us (0.64)
  blocking collectives: 95.8 us -> 0 us
  other arithmetic: 34.5 us -> 0.83 us
  waiting for transfers between devices: 0.01 us -> 32.2 us
  starting transfers between devices: 3.83 us -> 34.6 us
  Pallas kernels: 0 us -> 26 us
  matrix products: 9.91 us -> 0 us
  local copies, waits for them, and re-layouts: 5.78 us -> 2.42 us
    all_to_all x2 -> x0, blocking collectives: 95.8 us -> none  [the longest x1 68.5 us: on_device(): lax.all_to_all(lax.all_to_all(spectra, 'tblk', split_axis=0, concat_axis=...]
    pallas_call x0 -> x7, Pallas kernels: none -> 26 us  [the longest x1 9.16 us: on_device(): call(main_frames, (BLKS // 2,), [SMEM, pl.BlockSpec((16, 2 * quarter), la...]
    another operation x2 -> x5, other arithmetic: 24.7 us -> 0.83 us  [the longest x1 0.76 us: on_device(): far = along_ring(jnp.stack([far, other[3, 0]]), 4)]
    ppermute x1 -> x13, starting transfers between devices: 3.83 us -> 25.9 us  [the longest x9 14 us: along(): lax.ppermute(block, axis, [(i, (i + distance) % size) for i in range(size)])]
    ppermute x1 -> x13, waiting for transfers between devices: 0.01 us -> 19.1 us  [the longest x9 19.1 us: along(): lax.ppermute(block, axis, [(i, (i + distance) % size) for i in range(size)])]
    all_to_all x0 -> x1, waiting for transfers between devices: none -> 13.1 us  [on_device(): main = lax.all_to_all(main, AXES, split_axis=0, concat_axis=0, tiled=True)]
    dot_general x5 -> x0, matrix products: 9.91 us -> none  [the longest x4 5.13 us: products(): lax.dot_general(left_side, right_side, (((1,), (1,)), ((), ())), preferre...]
    all_to_all x0 -> x1, starting transfers between devices: none -> 8.67 us  [on_device(): main = lax.all_to_all(main, AXES, split_axis=0, concat_axis=0, tiled=True)]
  transfers between devices with their start and end apart: 1 -> 14, of which waited for: 0 -> 8; matrix products, arithmetic and copies ran while one was open for 13% -> 2% of each run, Pallas kernels for 0% -> 10%
where the time goes in v2:
time: 96.6 us; the launch traced here: 96.2 us
  starting transfers between devices  34.6 us (36%)
  waiting for transfers between devices  32.2 us (33%)
  Pallas kernels  26 us (27%)
  local copies, waits for them, and re-layouts  2.42 us (3%)
    ppermute x9, waiting for transfers between devices, along(): lax.ppermute(block, axis, [(i, (i + distance) % size) for i in range(size)])  19.1 us
    ppermute x9, starting transfers between devices, along(): lax.ppermute(block, axis, [(i, (i + distance) % size) for i in range(size)])  14 us
    all_to_all x1, waiting for transfers between devices, on_device(): main = lax.all_to_all(main, AXES, split_axis=0, concat_axis=0, tiled=True)  13.1 us
    ppermute x4, starting transfers between devices, along_ring(): return lax.ppermute(block, ('z', 'c'), route)  11.9 us
    pallas_call x1, Pallas kernels, on_device(): call(main_frames, (BLKS // 2,), [SMEM, pl.BlockSpec((16, 2 * quarter), la...  9.16 us
    all_to_all x1, starting transfers between devices, on_device(): main = lax.all_to_all(main, AXES, split_axis=0, concat_axis=0, tiled=True)  8.67 us
    pallas_call x1, Pallas kernels, on_device(): call(functools.partial(correlate, scale), (2, inputs // block), [whole(*p...  7.67 us
    pallas_call x1, Pallas kernels, on_device(): call(last_frames, (BLKS // 2,), [SMEM, SMEM, SMEM, SMEM, pl.BlockSpec((16...  7.32 us
  transfers between devices with their start and end apart: 14, of which 8 were waited for; matrix products, arithmetic and copies ran while one was open for 2% of the time, Pallas kernels for 10%

profile of v2, /device:TPU:1, one launch (start us, length us, event | category | flops | bytes accessed | tf_op | source)
XLA Modules:
  0.0 96.2 jit_solution(14955778479778919727)
XLA Ops:
  0.0 7.3 %last_frames.1 = (bf16[3,2,16,8,128]{4,3,2,1,0:T(8,128)(2,1)}, bf16[4,2,16,8,128]{4,3,2,1,0:T(8,128)(2,1)}, bf16[16,8,128]{2,1,0:T(8,128)(2,1)}, bf16[16,8,128]{2,1,0:T(8,128)(2,1)}, bf16[4,8,8,8,128]{4,3,2,1,0:T(8,128)(2,1)}) custom-call(s32[1]{0:T(128)} %bitcast.y_ref, s32[1]{0:T(128)} %bitcast.1.z_ref, s32[1]{0:T(128)} %bitcast.2.c_ref, f32[8]{0:T(128)} %gain_ref.2, ...), custom_call_target="tpu_custom_call" | custom-call | tf_op jit(solution)/shard_map/last_frames/pallas_call | solution.py:360
  7.3 3.3 %collective-permute-start = (bf16[4,2,16,8,128]{4,3,2,1,0:T(8,128)(2,1)}, bf16[4,2,16,8,128]{4,3,2,1,0:T(8,128)(2,1)S(1)}, u32[]{:S(2)}, u32[]{:S(2)}) collective-permute-start(bf16[4,2,16,8,128]{4,3,2,1,0:T(8,128)(2,1)} %get-tuple-element.27), channel_id=1, source_target_pairs={{0,1},{1,0},{2,3},{3,2},{4,5},{5,4},{6,7},{7,6},{8,9},{9,8},{10,11... | collective-permute-start | bytes 786440 | tf_op jit(solution)/shard_map/ppermute | solution.py:317
  10.7 1.2 %collective-permute-start.5 = (bf16[4,8,8,8,128]{4,3,2,1,0:T(8,128)(2,1)}, bf16[4,8,8,8,128]{4,3,2,1,0:T(8,128)(2,1)S(1)}, u32[]{:S(2)}, u32[]{:S(2)}) collective-permute-start(bf16[4,8,8,8,128]{4,3,2,1,0:T(8,128)(2,1)} %get-tuple-element.30), channel_id=1, source_target_pairs={{0,128},{128,0},{1,129},{129,1},{2,130},{130,2},{3,131},{131,3},{4... | collective-permute-start | bytes 1572872 | tf_op jit(solution)/shard_map/ppermute | solution.py:317
  11.9 0.9 slice_bitcast_fusion.1
  12.8 0.0 collective-permute-done
  12.8 5.7 %collective-permute-start.1 = (bf16[2,2,16,8,128]{4,3,2,0,1:T(8,128)(2,1)S(1)}, bf16[2,2,16,8,128]{4,3,2,0,1:T(8,128)(2,1)S(1)}, u32[]{:S(2)}, u32[]{:S(2)}) collective-permute-start(bf16[2,2,16,8,128]{4,3,2,0,1:T(8,128)(2,1)S(1)} %pad_maximum_fusion.1), channel_id=1, source_target_pairs={{0,8},{1,57},{8,16},{9,1},{16,24},{17,9},{24,32},{25,17},{32,40},{... | collective-permute-start | bytes 393224 | tf_op jit(solution)/shard_map/ppermute | solution.py:313
  18.5 1.2 %collective-permute-start.2 = (bf16[2,2,16,8,128]{4,3,2,0,1:T(8,128)(2,1)S(1)}, bf16[2,2,16,8,128]{4,3,2,0,1:T(8,128)(2,1)S(1)}, u32[]{:S(2)}, u32[]{:S(2)}) collective-permute-start(bf16[2,2,16,8,128]{4,3,2,0,1:T(8,128)(2,1)S(1)} %pad_maximum_fusion.2), channel_id=1, source_target_pairs={{0,16},{1,49},{8,24},{9,57},{16,32},{17,1},{24,40},{25,9},{32,48},... | collective-permute-start | bytes 393224 | tf_op jit(solution)/shard_map/ppermute | solution.py:313
  19.8 0.5 collective-permute-start.3
  20.3 0.8 pad_maximum_fusion.4
  21.1 4.5 %collective-permute-start.4 = (bf16[2,16,8,128]{3,2,1,0:T(8,128)(2,1)S(1)}, bf16[2,16,8,128]{3,2,1,0:T(8,128)(2,1)S(1)}, u32[]{:S(2)}, u32[]{:S(2)}) collective-permute-start(bf16[2,16,8,128]{3,2,1,0:T(8,128)(2,1)S(1)} %pad_maximum_fusion.4), channel_id=1, source_target_pairs={{0,32},{1,33},{8,40},{9,41},{16,48},{17,49},{24,56},{25,57},{32,0}... | collective-permute-start | bytes 196616 | tf_op jit(solution)/shard_map/ppermute | solution.py:313
  25.5 9.2 %main_frames.1 = bf16[3,4,8,8,8,128]{5,4,3,2,1,0:T(8,128)(2,1)} custom-call(f32[8]{0:T(128)} %gain_ref.2, bf16[64,32768]{1,0:T(8,128)(2,1)} %bitcast.28, bf16[64,32768]{1,0:T(8,128)(2,1)} %bitcast.29, f32[4,2048]{1,0:T(4,128)} %constant.38.clone.coef_ref, bf16[4,256,1024]{2,1,0:T(8,128)(2,1)} %constant.39.clone.table_ref), custom_call_target="tpu_custom_call" | custom-call | tf_op jit(solution)/shard_map/main_frames/pallas_call | solution.py:383
  34.7 0.0 collective-permute-done.4.far_ref
  34.7 0.0 collective-permute-done.1
  34.7 0.0 collective-permute-done.2
  34.8 0.0 collective-permute-done.3
  34.8 0.0 collective-permute-done.5
  34.8 0.0 copy-start
  34.8 1.4 %copy-done = bf16[3,4,8,8,8,128]{5,4,3,2,1,0:T(8,128)(2,1)S(1)} copy-done((bf16[3,4,8,8,8,128]{5,4,3,2,1,0:T(8,128)(2,1)S(1)}, bf16[3,4,8,8,8,128]{5,4,3,2,1,0:T(8,128)(2,1)}, u32[]{:S(2)}) %copy-start) | copy-done | bytes 1572888
  36.2 1.4 %complete.1 = bf16[256,3,8,128]{3,2,1,0:T(8,128)(2,1)} custom-call(bf16[3,256,8,128]{3,2,1,0:T(8,128)(2,1)S(1)} %bitcast.24, bf16[256,8,128]{2,1,0:T(8,128)(2,1)S(1)} %bitcast.25), custom_call_target="tpu_custom_call" | custom-call | tf_op jit(solution)/shard_map/complete/pallas_call | solution.py:336
  37.6 0.0 copy-start.1
  37.6 8.7 %all-to-all-start = ((bf16[256,3,8,128]{3,2,1,0:T(8,128)(2,1)}), bf16[256,3,8,128]{3,2,1,0:T(8,128)(2,1)S(1)}, u32[]{:S(2)}, u32[]{:S(2)}) async-start(bf16[256,3,8,128]{3,2,1,0:T(8,128)(2,1)} %complete.1), calls=%async_computation | async-start | bytes 3145728 | tf_op jit(solution)/shard_map/all_to_all | solution.py:404
  46.4 2.2 %collective-permute-start.6 = (bf16[3,2,16,8,128]{4,3,2,0,1:T(8,128)(2,1)S(1)}, bf16[3,2,16,8,128]{4,3,2,0,1:T(8,128)(2,1)S(1)}, u32[]{:S(2)}, u32[]{:S(2)}) collective-permute-start(bf16[3,2,16,8,128]{4,3,2,0,1:T(8,128)(2,1)S(1)} %pad_maximum_fusion), channel_id=1, source_target_pairs={{0,1},{1,0},{2,3},{3,2},{4,5},{5,4},{6,7},{7,6},{8,9},{9,8},{10,11... | collective-permute-start | bytes 589832 | tf_op jit(solution)/shard_map/ppermute | solution.py:317
  48.6 1.0 %collective-permute-done.6 = bf16[3,2,16,8,128]{4,3,2,0,1:T(8,128)(2,1)S(1)} collective-permute-done((bf16[3,2,16,8,128]{4,3,2,0,1:T(8,128)(2,1)S(1)}, bf16[3,2,16,8,128]{4,3,2,0,1:T(8,128)(2,1)S(1)}, u32[]{:S(2)}, u32[]{:S(2)}) %collective-permute-start.6) | collective-permute-done | bytes 196640 | tf_op jit(solution)/shard_map/ppermute | solution.py:317
  49.7 0.0 copy-done.1
  49.7 0.1 collective-permute-start.7
  49.8 2.0 %collective-permute-start.8 = (bf16[16,4,8,128]{3,2,1,0:T(8,128)(2,1)S(1)}, bf16[16,4,8,128]{3,2,1,0:T(8,128)(2,1)S(1)}, u32[]{:S(2)}, u32[]{:S(2)}) collective-permute-start(bf16[16,4,8,128]{3,2,1,0:T(8,128)(2,1)S(1)} %get-tuple-element.41), channel_id=1, source_target_pairs={{0,128},{64,192},{128,0},{192,64},{1,129},{65,193},{129,1},{193,65... | collective-permute-start | bytes 393224 | tf_op jit(solution)/shard_map/ppermute | solution.py:317
  51.9 1.1 %collective-permute-start.9 = (bf16[16,4,8,128]{3,2,1,0:T(8,128)(2,1)S(1)}, bf16[16,4,8,128]{3,2,1,0:T(8,128)(2,1)S(1)}, u32[]{:S(2)}, u32[]{:S(2)}) collective-permute-start(bf16[16,4,8,128]{3,2,1,0:T(8,128)(2,1)S(1)} %get-tuple-element.42), channel_id=1, source_target_pairs={{0,192},{64,0},{128,64},{192,128},{1,193},{65,1},{129,65},{193,129... | collective-permute-start | bytes 393224 | tf_op jit(solution)/shard_map/ppermute | solution.py:317
  53.0 5.5 %collective-permute-done.7.a1_ref = bf16[16,4,8,128]{3,2,1,0:T(8,128)(2,1)S(1)} collective-permute-done((bf16[16,4,8,128]{3,2,1,0:T(8,128)(2,1)S(1)}, bf16[16,4,8,128]{3,2,1,0:T(8,128)(2,1)S(1)}, u32[]{:S(2)}, u32[]{:S(2)}) %collective-permute-start.7) | collective-permute-done | bytes 131104 | tf_op jit(solution)/shard_map/ppermute | solution.py:317
  58.5 3.3 %collective-permute-done.8.a2_ref = bf16[16,4,8,128]{3,2,1,0:T(8,128)(2,1)S(1)} collective-permute-done((bf16[16,4,8,128]{3,2,1,0:T(8,128)(2,1)S(1)}, bf16[16,4,8,128]{3,2,1,0:T(8,128)(2,1)S(1)}, u32[]{:S(2)}, u32[]{:S(2)}) %collective-permute-start.8) | collective-permute-done | bytes 131104 | tf_op jit(solution)/shard_map/ppermute | solution.py:317
  61.8 1.1 %collective-permute-done.9.a3_ref = bf16[16,4,8,128]{3,2,1,0:T(8,128)(2,1)S(1)} collective-permute-done((bf16[16,4,8,128]{3,2,1,0:T(8,128)(2,1)S(1)}, bf16[16,4,8,128]{3,2,1,0:T(8,128)(2,1)S(1)}, u32[]{:S(2)}, u32[]{:S(2)}) %collective-permute-start.9) | collective-permute-done | bytes 131104 | tf_op jit(solution)/shard_map/ppermute | solution.py:317
  62.9 0.1 sort_x.1
  63.0 0.2 collective-permute-start.10
  63.2 2.4 %collective-permute-start.11 = (bf16[4,16,8,128]{3,2,1,0:T(8,128)(2,1)S(1)}, bf16[4,16,8,128]{3,2,1,0:T(8,128)(2,1)S(1)}, u32[]{:S(2)}, u32[]{:S(2)}) collective-permute-start(bf16[4,16,8,128]{3,2,1,0:T(8,128)(2,1)S(1)} %get-tuple-element.45), channel_id=1, source_target_pairs={{0,4},{2,6},{4,0},{6,2},{1,5},{3,7},{5,1},{7,3},{8,12},{10,14},{12... | collective-permute-start | bytes 393224 | tf_op jit(solution)/shard_map/ppermute | solution.py:317
  65.6 1.4 %collective-permute-start.12 = (bf16[4,16,8,128]{3,2,1,0:T(8,128)(2,1)S(1)}, bf16[4,16,8,128]{3,2,1,0:T(8,128)(2,1)S(1)}, u32[]{:S(2)}, u32[]{:S(2)}) collective-permute-start(bf16[4,16,8,128]{3,2,1,0:T(8,128)(2,1)S(1)} %get-tuple-element.46), channel_id=1, source_target_pairs={{0,6},{2,0},{4,2},{6,4},{1,7},{3,1},{5,3},{7,5},{8,14},{10,8},{12,... | collective-permute-start | bytes 393224 | tf_op jit(solution)/shard_map/ppermute | solution.py:317
  67.0 2.6 %collective-permute-done.10.a1_ref = bf16[4,16,8,128]{3,2,1,0:T(8,128)(2,1)S(1)} collective-permute-done((bf16[4,16,8,128]{3,2,1,0:T(8,128)(2,1)S(1)}, bf16[4,16,8,128]{3,2,1,0:T(8,128)(2,1)S(1)}, u32[]{:S(2)}, u32[]{:S(2)}) %collective-permute-start.10) | collective-permute-done | bytes 131104 | tf_op jit(solution)/shard_map/ppermute | solution.py:317
  69.6 5.1 %collective-permute-done.11.a2_ref = bf16[4,16,8,128]{3,2,1,0:T(8,128)(2,1)S(1)} collective-permute-done((bf16[4,16,8,128]{3,2,1,0:T(8,128)(2,1)S(1)}, bf16[4,16,8,128]{3,2,1,0:T(8,128)(2,1)S(1)}, u32[]{:S(2)}, u32[]{:S(2)}) %collective-permute-start.11) | collective-permute-done | bytes 131104 | tf_op jit(solution)/shard_map/ppermute | solution.py:317
  74.7 0.5 collective-permute-done.12.a3_ref
  75.2 0.3 arrange.1.last_ref
  75.4 13.1 %all-to-all-done.main_ref = bf16[256,3,8,128]{3,2,1,0:T(8,128)(2,1)S(1)} async-done(((bf16[256,3,8,128]{3,2,1,0:T(8,128)(2,1)}), bf16[256,3,8,128]{3,2,1,0:T(8,128)(2,1)S(1)}, u32[]{:S(2)}, u32[]{:S(2)}) %all-to-all-start) | async-done | bytes 1572896 | tf_op jit(solution)/shard_map/all_to_all | solution.py:404
  88.5 7.7 %correlate.1 = bf16[2,2,1024,1024]{3,2,1,0:T(8,128)(2,1)} custom-call(bf16[256,3,8,128]{3,2,1,0:T(8,128)(2,1)S(1)} %all-to-all-done.main_ref, bf16[256,8,128]{2,1,0:T(8,128)(2,1)S(1)} %arrange.1.last_ref), custom_call_target="tpu_custom_call" | custom-call | tf_op jit(solution)/shard_map/correlate/pallas_call | solution.py:418
  (13 shorter events, 0.2 us)
Async XLA Ops:
  7.3 5.4 %collective-permute-start = (bf16[4,2,16,8,128]{4,3,2,1,0:T(8,128)(2,1)}, bf16[4,2,16,8,128]{4,3,2,1,0:T(8,128)(2,1)S(1)}, u32[]{:S(2)}, u32[]{:S(2)}) collective-permute-start(bf16[4,2,16,8,128]{4,3,2,1,0:T(8,128)(2,1)} %get-tuple-element.27), channel_id=1, source_target_pairs={{0,1},{1,0},{2,3},{3,2},{4,5},{5,4},{6,7},{7,6},{8,9},{9,8},{10,11... | collective-permute-start | bytes 786440 | tf_op jit(solution)/shard_map/ppermute | solution.py:317
  10.7 24.1 %collective-permute-start.5 = (bf16[4,8,8,8,128]{4,3,2,1,0:T(8,128)(2,1)}, bf16[4,8,8,8,128]{4,3,2,1,0:T(8,128)(2,1)S(1)}, u32[]{:S(2)}, u32[]{:S(2)}) collective-permute-start(bf16[4,8,8,8,128]{4,3,2,1,0:T(8,128)(2,1)} %get-tuple-element.30), channel_id=1, source_target_pairs={{0,128},{128,0},{1,129},{129,1},{2,130},{130,2},{3,131},{131,3},{4... | collective-permute-start | bytes 1572872 | tf_op jit(solution)/shard_map/ppermute | solution.py:317
  12.8 21.9 %collective-permute-start.1 = (bf16[2,2,16,8,128]{4,3,2,0,1:T(8,128)(2,1)S(1)}, bf16[2,2,16,8,128]{4,3,2,0,1:T(8,128)(2,1)S(1)}, u32[]{:S(2)}, u32[]{:S(2)}) collective-permute-start(bf16[2,2,16,8,128]{4,3,2,0,1:T(8,128)(2,1)S(1)} %pad_maximum_fusion.1), channel_id=1, source_target_pairs={{0,8},{1,57},{8,16},{9,1},{16,24},{17,9},{24,32},{25,17},{32,40},{... | collective-permute-start | bytes 393224 | tf_op jit(solution)/shard_map/ppermute | solution.py:313
  18.5 16.2 %collective-permute-start.2 = (bf16[2,2,16,8,128]{4,3,2,0,1:T(8,128)(2,1)S(1)}, bf16[2,2,16,8,128]{4,3,2,0,1:T(8,128)(2,1)S(1)}, u32[]{:S(2)}, u32[]{:S(2)}) collective-permute-start(bf16[2,2,16,8,128]{4,3,2,0,1:T(8,128)(2,1)S(1)} %pad_maximum_fusion.2), channel_id=1, source_target_pairs={{0,16},{1,49},{8,24},{9,57},{16,32},{17,1},{24,40},{25,9},{32,48},... | collective-permute-start | bytes 393224 | tf_op jit(solution)/shard_map/ppermute | solution.py:313
  19.8 15.0 %collective-permute-start.3 = (bf16[2,2,16,8,128]{4,3,2,0,1:T(8,128)(2,1)S(1)}, bf16[2,2,16,8,128]{4,3,2,0,1:T(8,128)(2,1)S(1)}, u32[]{:S(2)}, u32[]{:S(2)}) collective-permute-start(bf16[2,2,16,8,128]{4,3,2,0,1:T(8,128)(2,1)S(1)} %pad_maximum_fusion.3), channel_id=1, source_target_pairs={{0,24},{1,41},{8,32},{9,49},{16,40},{17,57},{24,48},{25,1},{32,56}... | collective-permute-start | bytes 393224 | tf_op jit(solution)/shard_map/ppermute | solution.py:313
  21.1 13.6 %collective-permute-start.4 = (bf16[2,16,8,128]{3,2,1,0:T(8,128)(2,1)S(1)}, bf16[2,16,8,128]{3,2,1,0:T(8,128)(2,1)S(1)}, u32[]{:S(2)}, u32[]{:S(2)}) collective-permute-start(bf16[2,16,8,128]{3,2,1,0:T(8,128)(2,1)S(1)} %pad_maximum_fusion.4), channel_id=1, source_target_pairs={{0,32},{1,33},{8,40},{9,41},{16,48},{17,49},{24,56},{25,57},{32,0}... | collective-permute-start | bytes 196616 | tf_op jit(solution)/shard_map/ppermute | solution.py:313
  34.8 1.4 %copy-start = (bf16[3,4,8,8,8,128]{5,4,3,2,1,0:T(8,128)(2,1)S(1)}, bf16[3,4,8,8,8,128]{5,4,3,2,1,0:T(8,128)(2,1)}, u32[]{:S(2)}) copy-start(bf16[3,4,8,8,8,128]{5,4,3,2,1,0:T(8,128)(2,1)} %main_frames.1) | copy-start | bytes 4718596
  37.6 12.1 %copy-start.1 = (bf16[16,8,128]{2,1,0:T(8,128)(2,1)S(1)}, bf16[16,8,128]{2,1,0:T(8,128)(2,1)}, u32[]{:S(2)}) copy-start(bf16[16,8,128]{2,1,0:T(8,128)(2,1)} %get-tuple-element.38.near_ref) | copy-start | bytes 98308
  37.6 50.9 %all-to-all-start = ((bf16[256,3,8,128]{3,2,1,0:T(8,128)(2,1)}), bf16[256,3,8,128]{3,2,1,0:T(8,128)(2,1)S(1)}, u32[]{:S(2)}, u32[]{:S(2)}) async-start(bf16[256,3,8,128]{3,2,1,0:T(8,128)(2,1)} %complete.1), calls=%async_computation | async-start | bytes 3145728 | tf_op jit(solution)/shard_map/all_to_all | solution.py:404
  46.4 3.3 %collective-permute-start.6 = (bf16[3,2,16,8,128]{4,3,2,0,1:T(8,128)(2,1)S(1)}, bf16[3,2,16,8,128]{4,3,2,0,1:T(8,128)(2,1)S(1)}, u32[]{:S(2)}, u32[]{:S(2)}) collective-permute-start(bf16[3,2,16,8,128]{4,3,2,0,1:T(8,128)(2,1)S(1)} %pad_maximum_fusion), channel_id=1, source_target_pairs={{0,1},{1,0},{2,3},{3,2},{4,5},{5,4},{6,7},{7,6},{8,9},{9,8},{10,11... | collective-permute-start | bytes 589832 | tf_op jit(solution)/shard_map/ppermute | solution.py:317
  49.7 8.7 %collective-permute-start.7 = (bf16[16,4,8,128]{3,2,1,0:T(8,128)(2,1)S(1)}, bf16[16,4,8,128]{3,2,1,0:T(8,128)(2,1)S(1)}, u32[]{:S(2)}, u32[]{:S(2)}) collective-permute-start(bf16[16,4,8,128]{3,2,1,0:T(8,128)(2,1)S(1)} %get-tuple-element.40), channel_id=1, source_target_pairs={{0,64},{64,128},{128,192},{192,0},{1,65},{65,129},{129,193},{193,1... | collective-permute-start | bytes 393224 | tf_op jit(solution)/shard_map/ppermute | solution.py:317
  49.8 12.0 %collective-permute-start.8 = (bf16[16,4,8,128]{3,2,1,0:T(8,128)(2,1)S(1)}, bf16[16,4,8,128]{3,2,1,0:T(8,128)(2,1)S(1)}, u32[]{:S(2)}, u32[]{:S(2)}) collective-permute-start(bf16[16,4,8,128]{3,2,1,0:T(8,128)(2,1)S(1)} %get-tuple-element.41), channel_id=1, source_target_pairs={{0,128},{64,192},{128,0},{192,64},{1,129},{65,193},{129,1},{193,65... | collective-permute-start | bytes 393224 | tf_op jit(solution)/shard_map/ppermute | solution.py:317
  51.9 11.0 %collective-permute-start.9 = (bf16[16,4,8,128]{3,2,1,0:T(8,128)(2,1)S(1)}, bf16[16,4,8,128]{3,2,1,0:T(8,128)(2,1)S(1)}, u32[]{:S(2)}, u32[]{:S(2)}) collective-permute-start(bf16[16,4,8,128]{3,2,1,0:T(8,128)(2,1)S(1)} %get-tuple-element.42), channel_id=1, source_target_pairs={{0,192},{64,0},{128,64},{192,128},{1,193},{65,1},{129,65},{193,129... | collective-permute-start | bytes 393224 | tf_op jit(solution)/shard_map/ppermute | solution.py:317
  63.0 6.6 %collective-permute-start.10 = (bf16[4,16,8,128]{3,2,1,0:T(8,128)(2,1)S(1)}, bf16[4,16,8,128]{3,2,1,0:T(8,128)(2,1)S(1)}, u32[]{:S(2)}, u32[]{:S(2)}) collective-permute-start(bf16[4,16,8,128]{3,2,1,0:T(8,128)(2,1)S(1)} %get-tuple-element.44), channel_id=1, source_target_pairs={{0,2},{2,4},{4,6},{6,0},{1,3},{3,5},{5,7},{7,1},{8,10},{10,12},{12... | collective-permute-start | bytes 393224 | tf_op jit(solution)/shard_map/ppermute | solution.py:317
  63.2 11.5 %collective-permute-start.11 = (bf16[4,16,8,128]{3,2,1,0:T(8,128)(2,1)S(1)}, bf16[4,16,8,128]{3,2,1,0:T(8,128)(2,1)S(1)}, u32[]{:S(2)}, u32[]{:S(2)}) collective-permute-start(bf16[4,16,8,128]{3,2,1,0:T(8,128)(2,1)S(1)} %get-tuple-element.45), channel_id=1, source_target_pairs={{0,4},{2,6},{4,0},{6,2},{1,5},{3,7},{5,1},{7,3},{8,12},{10,14},{12... | collective-permute-start | bytes 393224 | tf_op jit(solution)/shard_map/ppermute | solution.py:317
  65.6 9.5 %collective-permute-start.12 = (bf16[4,16,8,128]{3,2,1,0:T(8,128)(2,1)S(1)}, bf16[4,16,8,128]{3,2,1,0:T(8,128)(2,1)S(1)}, u32[]{:S(2)}, u32[]{:S(2)}) collective-permute-start(bf16[4,16,8,128]{3,2,1,0:T(8,128)(2,1)S(1)} %get-tuple-element.46), channel_id=1, source_target_pairs={{0,6},{2,0},{4,2},{6,4},{1,7},{3,1},{5,3},{7,5},{8,14},{10,8},{12,... | collective-permute-start | bytes 393224 | tf_op jit(solution)/shard_map/ppermute | solution.py:317

commit v3 on v2

--- a/solution.py
+++ b/solution.py
@@ -330,6 +330,11 @@
 
 
 SMEM = pl.BlockSpec(memory_space=pltpu.SMEM)
+IN_VMEM = pl.BlockSpec(memory_space=pltpu.VMEM)
+
+
+def in_vmem(array):
+    return pltpu.with_memory_space_constraint(array, pltpu.VMEM)
 
 
 def simple(kernel, scalars, arrays, shapes, name):
@@ -364,7 +369,7 @@
             pl.BlockSpec((16, quarter), lambda g: (g, 3)),
             pl.BlockSpec((16, quarter), lambda g: (g, 2)),
         ] + tables,
-        [whole(*s) for s in last_shapes], [jax.ShapeDtypeStruct(s, BF16) for s in last_shapes],
+        [IN_VMEM] * 5, [pltpu.VMEM(s, BF16) for s in last_shapes],
         [
             pltpu.VMEM((2, HALF // LANES, 256, LANES), F32),
             pltpu.VMEM((2, HALF // LANES, (TAPS - 1) * 80, LANES), F32),
@@ -387,20 +392,21 @@
             pl.BlockSpec((16, 2 * quarter), lambda g: (g, 0)),
             pl.BlockSpec((16, quarter), lambda g: (g, 2)),
         ] + tables,
-        whole(3, *owners), jax.ShapeDtypeStruct((3,) + owners, BF16),
+        IN_VMEM, pltpu.VMEM((3,) + owners, BF16),
         [
             pltpu.VMEM((2, HALF // LANES, 768, LANES), F32),
             pltpu.VMEM((4, 768, HALF), BF16),
             pltpu.VMEM((4, DEVICES, 768), F32),
             pltpu.VMEM((3 * RING, FLAT * SUB, LANES), F32),
         ] + table_scratch,
-        "main_frames", 56,
+        "main_frames", 52,
     )(main_gains, stream, stream, coefs, table)
     ring, far, tail, main = lax.optimization_barrier((ring, far, tail, main))
     packed = (DEVICES, 3) + tile
-    main, = simple(
-        complete, (), (main.reshape((3, DEVICES) + tile), tail.reshape((DEVICES,) + tile)), [packed], "complete"
-    )
+    main = pl.pallas_call(
+        complete, in_specs=[IN_VMEM] * 2, out_specs=IN_VMEM, out_shape=pltpu.VMEM(packed, BF16), name="complete",
+        compiler_params=pltpu.CompilerParams(vmem_limit_bytes=8 * MIB),
+    )(in_vmem(main.reshape((3, DEVICES) + tile)), in_vmem(tail.reshape((DEVICES,) + tile)))
     main = lax.all_to_all(main, AXES, split_axis=0, concat_axis=0, tiled=True)
 
     leaving = jnp.stack([lax.dynamic_index_in_dim(a, 1 - core[0], 0, keepdims=False) for a in ring])

time: 96.6 us -> 92.1 us (0.953)
  local copies, waits for them, and re-layouts: 2.42 us -> 0.12 us
  Pallas kernels: 26 us -> 23.9 us
    pallas_call x0 -> x1, Pallas kernels: none -> 1.42 us  [on_device(): pl.pallas_call(complete, in_specs=[IN_VMEM] * 2, out_specs=IN_VMEM, out_s...]
    pallas_call x4 -> x3, Pallas kernels: 1.81 us -> 0.39 us  [simple(): call(kernel, (1,), [SMEM] * len(scalars) + [whole(*a.shape) for a in arra...]
    unnamed x4, local copies, waits for them, and re-layouts: 1.41 us -> 0.01 us
    pallas_call x1, Pallas kernels: 9.16 us -> 8.03 us  [on_device(): call(main_frames, (BLKS // 2,), [SMEM, pl.BlockSpec((16, 2 * quarter), la...]
  transfers between devices with their start and end apart: 14 -> 14, of which waited for: 8 -> 8; matrix products, arithmetic and copies ran while one was open for 2% -> 0% of each run, Pallas kernels for 10% -> 9%
where the time goes in v3:
time: 92.1 us; the launch traced here: 91.8 us
  starting transfers between devices  35.3 us (38%)
  waiting for transfers between devices  32.2 us (35%)
  Pallas kernels  23.9 us (26%)
    ppermute x9, waiting for transfers between devices, along(): lax.ppermute(block, axis, [(i, (i + distance) % size) for i in range(size)])  19.2 us
    ppermute x9, starting transfers between devices, along(): lax.ppermute(block, axis, [(i, (i + distance) % size) for i in range(size)])  14 us
    all_to_all x1, waiting for transfers between devices, on_device(): main = lax.all_to_all(main, AXES, split_axis=0, concat_axis=0, tiled=True)  13.1 us
    ppermute x4, starting transfers between devices, along_ring(): return lax.ppermute(block, ('z', 'c'), route)  12 us
    all_to_all x1, starting transfers between devices, on_device(): main = lax.all_to_all(main, AXES, split_axis=0, concat_axis=0, tiled=True)  9.35 us
    pallas_call x1, Pallas kernels, on_device(): call(main_frames, (BLKS // 2,), [SMEM, pl.BlockSpec((16, 2 * quarter), la...  8.03 us
    pallas_call x1, Pallas kernels, on_device(): call(functools.partial(correlate, scale), (2, inputs // block), [whole(*p...  7.68 us
    pallas_call x1, Pallas kernels, on_device(): call(last_frames, (BLKS // 2,), [SMEM, SMEM, SMEM, SMEM, pl.BlockSpec((16...  6.38 us
  transfers between devices with their start and end apart: 14, of which 8 were waited for; matrix products, arithmetic and copies ran while one was open for 0% of the time, Pallas kernels for 9%

profile of v3, /device:TPU:1, one launch (start us, length us, event | category | flops | bytes accessed | tf_op | source)
XLA Modules:
  0.0 91.8 jit_solution(6709165969228343794)
XLA Ops:
  0.0 0.0 copy-start
  0.0 0.0 copy-start.1
  0.0 6.4 %last_frames.1 = (bf16[3,2,16,8,128]{4,3,2,1,0:T(8,128)(2,1)S(1)}, bf16[4,2,16,8,128]{4,3,2,1,0:T(8,128)(2,1)S(1)}, bf16[16,8,128]{2,1,0:T(8,128)(2,1)S(1)}, bf1...) custom-call(s32[1]{0:T(128)} %bitcast.y_ref, s32[1]{0:T(128)} %bitcast.1.z_ref, s32[1]{0:T(128)} %bitcast.2.c_ref, ...), custom_call_target="tpu_custom_call" | custom-call | tf_op jit(solution)/shard_map/last_frames/pallas_call | solution.py:365
  6.4 3.3 %collective-permute-start = (bf16[4,2,16,8,128]{4,3,2,1,0:T(8,128)(2,1)S(1)}, bf16[4,2,16,8,128]{4,3,2,1,0:T(8,128)(2,1)S(1)}, u32[]{:S(2)}, u32[]{:S(2)}) collective-permute-start(bf16[4,2,16,8,128]{4,3,2,1,0:T(8,128)(2,1)S(1)} %get-tuple-element.27), channel_id=1, source_target_pairs={{0,1},{1,0},{2,3},{3,2},{4,5},{5,4},{6,7},{7,6},{8,9},{9,8},{10,11... | collective-permute-start | bytes 786440 | tf_op jit(solution)/shard_map/ppermute | solution.py:317
  9.7 1.2 %collective-permute-start.5 = (bf16[4,8,8,8,128]{4,3,2,1,0:T(8,128)(2,1)S(1)}, bf16[4,8,8,8,128]{4,3,2,1,0:T(8,128)(2,1)S(1)}, u32[]{:S(2)}, u32[]{:S(2)}) collective-permute-start(bf16[4,8,8,8,128]{4,3,2,1,0:T(8,128)(2,1)S(1)} %get-tuple-element.30), channel_id=1, source_target_pairs={{0,128},{128,0},{1,129},{129,1},{2,130},{130,2},{3,131},{131,3},{4... | collective-permute-start | bytes 1572872 | tf_op jit(solution)/shard_map/ppermute | solution.py:317
  10.9 0.0 collective-permute-done
  11.0 5.7 %collective-permute-start.1 = (bf16[2,2,16,8,128]{4,3,2,0,1:T(8,128)(2,1)S(1)}, bf16[2,2,16,8,128]{4,3,2,0,1:T(8,128)(2,1)S(1)}, u32[]{:S(2)}, u32[]{:S(2)}) collective-permute-start(bf16[2,2,16,8,128]{4,3,2,0,1:T(8,128)(2,1)S(1)} %pad_maximum_fusion.1), channel_id=1, source_target_pairs={{0,8},{1,57},{8,16},{9,1},{16,24},{17,9},{24,32},{25,17},{32,40},{... | collective-permute-start | bytes 393224 | tf_op jit(solution)/shard_map/ppermute | solution.py:313
  16.7 1.2 %collective-permute-start.2 = (bf16[2,2,16,8,128]{4,3,2,0,1:T(8,128)(2,1)S(1)}, bf16[2,2,16,8,128]{4,3,2,0,1:T(8,128)(2,1)S(1)}, u32[]{:S(2)}, u32[]{:S(2)}) collective-permute-start(bf16[2,2,16,8,128]{4,3,2,0,1:T(8,128)(2,1)S(1)} %pad_maximum_fusion.2), channel_id=1, source_target_pairs={{0,16},{1,49},{8,24},{9,57},{16,32},{17,1},{24,40},{25,9},{32,48},... | collective-permute-start | bytes 393224 | tf_op jit(solution)/shard_map/ppermute | solution.py:313
  17.9 0.5 collective-permute-start.3
  18.5 4.5 %collective-permute-start.4 = (bf16[2,16,8,128]{3,2,1,0:T(8,128)(2,1)S(1)}, bf16[2,16,8,128]{3,2,1,0:T(8,128)(2,1)S(1)}, u32[]{:S(2)}, u32[]{:S(2)}) collective-permute-start(bf16[2,16,8,128]{3,2,1,0:T(8,128)(2,1)S(1)} %pad_maximum_fusion.4), channel_id=1, source_target_pairs={{0,32},{1,33},{8,40},{9,41},{16,48},{17,49},{24,56},{25,57},{32,0}... | collective-permute-start | bytes 196616 | tf_op jit(solution)/shard_map/ppermute | solution.py:313
  23.0 0.0 copy-done
  23.0 0.0 copy-done.1
  23.0 8.0 %main_frames.1 = bf16[3,4,8,8,8,128]{5,4,3,2,1,0:T(8,128)(2,1)S(1)} custom-call(f32[8]{0:T(128)S(1)} %copy-done.1, bf16[64,32768]{1,0:T(8,128)(2,1)} %bitcast.29, bf16[64,32768]{1,0:T(8,128)(2,1)} %bitcast.30, f32[4,2048]{1,0:T(4,128)S(1)} %copy-done, bf16[4,256,1024]{2,1,0:T(8,128)(2,1)} %constant.39.clone.table_ref), custom_call_target="tpu_custom_call" | custom-call | tf_op jit(solution)/shard_map/main_frames/pallas_call | solution.py:388
  31.1 0.0 collective-permute-done.4.far_ref
  31.1 0.0 collective-permute-done.1
  31.1 0.0 collective-permute-done.2
  31.1 0.0 collective-permute-done.3
  31.1 0.0 collective-permute-done.5
  31.1 1.4 %complete.1 = bf16[256,3,8,128]{3,2,1,0:T(8,128)(2,1)} custom-call(bf16[3,256,8,128]{3,2,1,0:T(8,128)(2,1)S(1)} %bitcast.24, bf16[256,8,128]{2,1,0:T(8,128)(2,1)S(1)} %bitcast.25), custom_call_target="tpu_custom_call" | custom-call | tf_op jit(solution)/shard_map/complete/pallas_call | solution.py:406
  32.6 9.3 %all-to-all-start = ((bf16[256,3,8,128]{3,2,1,0:T(8,128)(2,1)}), bf16[256,3,8,128]{3,2,1,0:T(8,128)(2,1)S(1)}, u32[]{:S(2)}, u32[]{:S(2)}) async-start(bf16[256,3,8,128]{3,2,1,0:T(8,128)(2,1)} %complete.1), calls=%async_computation | async-start | bytes 3145728 | tf_op jit(solution)/shard_map/all_to_all | solution.py:410
  42.0 2.2 %collective-permute-start.6 = (bf16[3,2,16,8,128]{4,3,2,0,1:T(8,128)(2,1)S(1)}, bf16[3,2,16,8,128]{4,3,2,0,1:T(8,128)(2,1)S(1)}, u32[]{:S(2)}, u32[]{:S(2)}) collective-permute-start(bf16[3,2,16,8,128]{4,3,2,0,1:T(8,128)(2,1)S(1)} %pad_maximum_fusion), channel_id=1, source_target_pairs={{0,1},{1,0},{2,3},{3,2},{4,5},{5,4},{6,7},{7,6},{8,9},{9,8},{10,11... | collective-permute-start | bytes 589832 | tf_op jit(solution)/shard_map/ppermute | solution.py:317
  44.3 1.0 %collective-permute-done.6 = bf16[3,2,16,8,128]{4,3,2,0,1:T(8,128)(2,1)S(1)} collective-permute-done((bf16[3,2,16,8,128]{4,3,2,0,1:T(8,128)(2,1)S(1)}, bf16[3,2,16,8,128]{4,3,2,0,1:T(8,128)(2,1)S(1)}, u32[]{:S(2)}, u32[]{:S(2)}) %collective-permute-start.6) | collective-permute-done | bytes 196640 | tf_op jit(solution)/shard_map/ppermute | solution.py:317
  45.4 0.1 collective-permute-start.7
  45.5 2.0 %collective-permute-start.8 = (bf16[16,4,8,128]{3,2,1,0:T(8,128)(2,1)S(1)}, bf16[16,4,8,128]{3,2,1,0:T(8,128)(2,1)S(1)}, u32[]{:S(2)}, u32[]{:S(2)}) collective-permute-start(bf16[16,4,8,128]{3,2,1,0:T(8,128)(2,1)S(1)} %get-tuple-element.41), channel_id=1, source_target_pairs={{0,128},{64,192},{128,0},{192,64},{1,129},{65,193},{129,1},{193,65... | collective-permute-start | bytes 393224 | tf_op jit(solution)/shard_map/ppermute | solution.py:317
  47.5 1.1 %collective-permute-start.9 = (bf16[16,4,8,128]{3,2,1,0:T(8,128)(2,1)S(1)}, bf16[16,4,8,128]{3,2,1,0:T(8,128)(2,1)S(1)}, u32[]{:S(2)}, u32[]{:S(2)}) collective-permute-start(bf16[16,4,8,128]{3,2,1,0:T(8,128)(2,1)S(1)} %get-tuple-element.42), channel_id=1, source_target_pairs={{0,192},{64,0},{128,64},{192,128},{1,193},{65,1},{129,65},{193,129... | collective-permute-start | bytes 393224 | tf_op jit(solution)/shard_map/ppermute | solution.py:317
  48.6 5.5 %collective-permute-done.7.a1_ref = bf16[16,4,8,128]{3,2,1,0:T(8,128)(2,1)S(1)} collective-permute-done((bf16[16,4,8,128]{3,2,1,0:T(8,128)(2,1)S(1)}, bf16[16,4,8,128]{3,2,1,0:T(8,128)(2,1)S(1)}, u32[]{:S(2)}, u32[]{:S(2)}) %collective-permute-start.7) | collective-permute-done | bytes 131104 | tf_op jit(solution)/shard_map/ppermute | solution.py:317
  54.1 3.3 %collective-permute-done.8.a2_ref = bf16[16,4,8,128]{3,2,1,0:T(8,128)(2,1)S(1)} collective-permute-done((bf16[16,4,8,128]{3,2,1,0:T(8,128)(2,1)S(1)}, bf16[16,4,8,128]{3,2,1,0:T(8,128)(2,1)S(1)}, u32[]{:S(2)}, u32[]{:S(2)}) %collective-permute-start.8) | collective-permute-done | bytes 131104 | tf_op jit(solution)/shard_map/ppermute | solution.py:317
  57.4 1.1 %collective-permute-done.9.a3_ref = bf16[16,4,8,128]{3,2,1,0:T(8,128)(2,1)S(1)} collective-permute-done((bf16[16,4,8,128]{3,2,1,0:T(8,128)(2,1)S(1)}, bf16[16,4,8,128]{3,2,1,0:T(8,128)(2,1)S(1)}, u32[]{:S(2)}, u32[]{:S(2)}) %collective-permute-start.9) | collective-permute-done | bytes 131104 | tf_op jit(solution)/shard_map/ppermute | solution.py:317
  58.5 0.1 sort_x.1
  58.6 0.2 collective-permute-start.10
  58.8 2.4 %collective-permute-start.11 = (bf16[4,16,8,128]{3,2,1,0:T(8,128)(2,1)S(1)}, bf16[4,16,8,128]{3,2,1,0:T(8,128)(2,1)S(1)}, u32[]{:S(2)}, u32[]{:S(2)}) collective-permute-start(bf16[4,16,8,128]{3,2,1,0:T(8,128)(2,1)S(1)} %get-tuple-element.45), channel_id=1, source_target_pairs={{0,4},{2,6},{4,0},{6,2},{1,5},{3,7},{5,1},{7,3},{8,12},{10,14},{12... | collective-permute-start | bytes 393224 | tf_op jit(solution)/shard_map/ppermute | solution.py:317
  61.2 1.3 %collective-permute-start.12 = (bf16[4,16,8,128]{3,2,1,0:T(8,128)(2,1)S(1)}, bf16[4,16,8,128]{3,2,1,0:T(8,128)(2,1)S(1)}, u32[]{:S(2)}, u32[]{:S(2)}) collective-permute-start(bf16[4,16,8,128]{3,2,1,0:T(8,128)(2,1)S(1)} %get-tuple-element.46), channel_id=1, source_target_pairs={{0,6},{2,0},{4,2},{6,4},{1,7},{3,1},{5,3},{7,5},{8,14},{10,8},{12,... | collective-permute-start | bytes 393224 | tf_op jit(solution)/shard_map/ppermute | solution.py:317
  62.6 2.6 %collective-permute-done.10.a1_ref = bf16[4,16,8,128]{3,2,1,0:T(8,128)(2,1)S(1)} collective-permute-done((bf16[4,16,8,128]{3,2,1,0:T(8,128)(2,1)S(1)}, bf16[4,16,8,128]{3,2,1,0:T(8,128)(2,1)S(1)}, u32[]{:S(2)}, u32[]{:S(2)}) %collective-permute-start.10) | collective-permute-done | bytes 131104 | tf_op jit(solution)/shard_map/ppermute | solution.py:317
  65.2 5.0 %collective-permute-done.11.a2_ref = bf16[4,16,8,128]{3,2,1,0:T(8,128)(2,1)S(1)} collective-permute-done((bf16[4,16,8,128]{3,2,1,0:T(8,128)(2,1)S(1)}, bf16[4,16,8,128]{3,2,1,0:T(8,128)(2,1)S(1)}, u32[]{:S(2)}, u32[]{:S(2)}) %collective-permute-start.11) | collective-permute-done | bytes 131104 | tf_op jit(solution)/shard_map/ppermute | solution.py:317
  70.3 0.6 collective-permute-done.12.a3_ref
  70.8 0.3 arrange.1.last_ref
  71.1 13.1 %all-to-all-done.main_ref = bf16[256,3,8,128]{3,2,1,0:T(8,128)(2,1)S(1)} async-done(((bf16[256,3,8,128]{3,2,1,0:T(8,128)(2,1)}), bf16[256,3,8,128]{3,2,1,0:T(8,128)(2,1)S(1)}, u32[]{:S(2)}, u32[]{:S(2)}) %all-to-all-start) | async-done | bytes 1572896 | tf_op jit(solution)/shard_map/all_to_all | solution.py:410
  84.2 7.7 %correlate.1 = bf16[2,2,1024,1024]{3,2,1,0:T(8,128)(2,1)} custom-call(bf16[256,3,8,128]{3,2,1,0:T(8,128)(2,1)S(1)} %all-to-all-done.main_ref, bf16[256,8,128]{2,1,0:T(8,128)(2,1)S(1)} %arrange.1.last_ref), custom_call_target="tpu_custom_call" | custom-call | tf_op jit(solution)/shard_map/correlate/pallas_call | solution.py:424
  (15 shorter events, 0.2 us)
Async XLA Ops:
  0.0 23.0 %copy-start = (f32[4,2048]{1,0:T(4,128)S(1)}, f32[4,2048]{1,0:T(4,128)}, u32[]{:S(2)}) copy-start(f32[4,2048]{1,0:T(4,128)} %constant.38.clone.coef_ref) | copy-start | bytes 98308
  0.0 23.0 %copy-start.1 = (f32[8]{0:T(128)S(1)}, f32[8]{0:T(128)}, u32[]{:S(2)}) copy-start(f32[8]{0:T(128)} %gain_ref.2) | copy-start | bytes 100
  6.4 4.5 %collective-permute-start = (bf16[4,2,16,8,128]{4,3,2,1,0:T(8,128)(2,1)S(1)}, bf16[4,2,16,8,128]{4,3,2,1,0:T(8,128)(2,1)S(1)}, u32[]{:S(2)}, u32[]{:S(2)}) collective-permute-start(bf16[4,2,16,8,128]{4,3,2,1,0:T(8,128)(2,1)S(1)} %get-tuple-element.27), channel_id=1, source_target_pairs={{0,1},{1,0},{2,3},{3,2},{4,5},{5,4},{6,7},{7,6},{8,9},{9,8},{10,11... | collective-permute-start | bytes 786440 | tf_op jit(solution)/shard_map/ppermute | solution.py:317
  9.7 21.4 %collective-permute-start.5 = (bf16[4,8,8,8,128]{4,3,2,1,0:T(8,128)(2,1)S(1)}, bf16[4,8,8,8,128]{4,3,2,1,0:T(8,128)(2,1)S(1)}, u32[]{:S(2)}, u32[]{:S(2)}) collective-permute-start(bf16[4,8,8,8,128]{4,3,2,1,0:T(8,128)(2,1)S(1)} %get-tuple-element.30), channel_id=1, source_target_pairs={{0,128},{128,0},{1,129},{129,1},{2,130},{130,2},{3,131},{131,3},{4... | collective-permute-start | bytes 1572872 | tf_op jit(solution)/shard_map/ppermute | solution.py:317
  11.0 20.1 %collective-permute-start.1 = (bf16[2,2,16,8,128]{4,3,2,0,1:T(8,128)(2,1)S(1)}, bf16[2,2,16,8,128]{4,3,2,0,1:T(8,128)(2,1)S(1)}, u32[]{:S(2)}, u32[]{:S(2)}) collective-permute-start(bf16[2,2,16,8,128]{4,3,2,0,1:T(8,128)(2,1)S(1)} %pad_maximum_fusion.1), channel_id=1, source_target_pairs={{0,8},{1,57},{8,16},{9,1},{16,24},{17,9},{24,32},{25,17},{32,40},{... | collective-permute-start | bytes 393224 | tf_op jit(solution)/shard_map/ppermute | solution.py:313
  16.7 14.4 %collective-permute-start.2 = (bf16[2,2,16,8,128]{4,3,2,0,1:T(8,128)(2,1)S(1)}, bf16[2,2,16,8,128]{4,3,2,0,1:T(8,128)(2,1)S(1)}, u32[]{:S(2)}, u32[]{:S(2)}) collective-permute-start(bf16[2,2,16,8,128]{4,3,2,0,1:T(8,128)(2,1)S(1)} %pad_maximum_fusion.2), channel_id=1, source_target_pairs={{0,16},{1,49},{8,24},{9,57},{16,32},{17,1},{24,40},{25,9},{32,48},... | collective-permute-start | bytes 393224 | tf_op jit(solution)/shard_map/ppermute | solution.py:313
  17.9 13.2 %collective-permute-start.3 = (bf16[2,2,16,8,128]{4,3,2,0,1:T(8,128)(2,1)S(1)}, bf16[2,2,16,8,128]{4,3,2,0,1:T(8,128)(2,1)S(1)}, u32[]{:S(2)}, u32[]{:S(2)}) collective-permute-start(bf16[2,2,16,8,128]{4,3,2,0,1:T(8,128)(2,1)S(1)} %pad_maximum_fusion.3), channel_id=1, source_target_pairs={{0,24},{1,41},{8,32},{9,49},{16,40},{17,57},{24,48},{25,1},{32,56}... | collective-permute-start | bytes 393224 | tf_op jit(solution)/shard_map/ppermute | solution.py:313
  18.5 12.6 %collective-permute-start.4 = (bf16[2,16,8,128]{3,2,1,0:T(8,128)(2,1)S(1)}, bf16[2,16,8,128]{3,2,1,0:T(8,128)(2,1)S(1)}, u32[]{:S(2)}, u32[]{:S(2)}) collective-permute-start(bf16[2,16,8,128]{3,2,1,0:T(8,128)(2,1)S(1)} %pad_maximum_fusion.4), channel_id=1, source_target_pairs={{0,32},{1,33},{8,40},{9,41},{16,48},{17,49},{24,56},{25,57},{32,0}... | collective-permute-start | bytes 196616 | tf_op jit(solution)/shard_map/ppermute | solution.py:313
  32.6 51.6 %all-to-all-start = ((bf16[256,3,8,128]{3,2,1,0:T(8,128)(2,1)}), bf16[256,3,8,128]{3,2,1,0:T(8,128)(2,1)S(1)}, u32[]{:S(2)}, u32[]{:S(2)}) async-start(bf16[256,3,8,128]{3,2,1,0:T(8,128)(2,1)} %complete.1), calls=%async_computation | async-start | bytes 3145728 | tf_op jit(solution)/shard_map/all_to_all | solution.py:410
  42.0 3.3 %collective-permute-start.6 = (bf16[3,2,16,8,128]{4,3,2,0,1:T(8,128)(2,1)S(1)}, bf16[3,2,16,8,128]{4,3,2,0,1:T(8,128)(2,1)S(1)}, u32[]{:S(2)}, u32[]{:S(2)}) collective-permute-start(bf16[3,2,16,8,128]{4,3,2,0,1:T(8,128)(2,1)S(1)} %pad_maximum_fusion), channel_id=1, source_target_pairs={{0,1},{1,0},{2,3},{3,2},{4,5},{5,4},{6,7},{7,6},{8,9},{9,8},{10,11... | collective-permute-start | bytes 589832 | tf_op jit(solution)/shard_map/ppermute | solution.py:317
  45.4 8.8 %collective-permute-start.7 = (bf16[16,4,8,128]{3,2,1,0:T(8,128)(2,1)S(1)}, bf16[16,4,8,128]{3,2,1,0:T(8,128)(2,1)S(1)}, u32[]{:S(2)}, u32[]{:S(2)}) collective-permute-start(bf16[16,4,8,128]{3,2,1,0:T(8,128)(2,1)S(1)} %get-tuple-element.40), channel_id=1, source_target_pairs={{0,64},{64,128},{128,192},{192,0},{1,65},{65,129},{129,193},{193,1... | collective-permute-start | bytes 393224 | tf_op jit(solution)/shard_map/ppermute | solution.py:317
  45.5 12.0 %collective-permute-start.8 = (bf16[16,4,8,128]{3,2,1,0:T(8,128)(2,1)S(1)}, bf16[16,4,8,128]{3,2,1,0:T(8,128)(2,1)S(1)}, u32[]{:S(2)}, u32[]{:S(2)}) collective-permute-start(bf16[16,4,8,128]{3,2,1,0:T(8,128)(2,1)S(1)} %get-tuple-element.41), channel_id=1, source_target_pairs={{0,128},{64,192},{128,0},{192,64},{1,129},{65,193},{129,1},{193,65... | collective-permute-start | bytes 393224 | tf_op jit(solution)/shard_map/ppermute | solution.py:317
  47.5 11.0 %collective-permute-start.9 = (bf16[16,4,8,128]{3,2,1,0:T(8,128)(2,1)S(1)}, bf16[16,4,8,128]{3,2,1,0:T(8,128)(2,1)S(1)}, u32[]{:S(2)}, u32[]{:S(2)}) collective-permute-start(bf16[16,4,8,128]{3,2,1,0:T(8,128)(2,1)S(1)} %get-tuple-element.42), channel_id=1, source_target_pairs={{0,192},{64,0},{128,64},{192,128},{1,193},{65,1},{129,65},{193,129... | collective-permute-start | bytes 393224 | tf_op jit(solution)/shard_map/ppermute | solution.py:317
  58.6 6.6 %collective-permute-start.10 = (bf16[4,16,8,128]{3,2,1,0:T(8,128)(2,1)S(1)}, bf16[4,16,8,128]{3,2,1,0:T(8,128)(2,1)S(1)}, u32[]{:S(2)}, u32[]{:S(2)}) collective-permute-start(bf16[4,16,8,128]{3,2,1,0:T(8,128)(2,1)S(1)} %get-tuple-element.44), channel_id=1, source_target_pairs={{0,2},{2,4},{4,6},{6,0},{1,3},{3,5},{5,7},{7,1},{8,10},{10,12},{12... | collective-permute-start | bytes 393224 | tf_op jit(solution)/shard_map/ppermute | solution.py:317
  58.8 11.5 %collective-permute-start.11 = (bf16[4,16,8,128]{3,2,1,0:T(8,128)(2,1)S(1)}, bf16[4,16,8,128]{3,2,1,0:T(8,128)(2,1)S(1)}, u32[]{:S(2)}, u32[]{:S(2)}) collective-permute-start(bf16[4,16,8,128]{3,2,1,0:T(8,128)(2,1)S(1)} %get-tuple-element.45), channel_id=1, source_target_pairs={{0,4},{2,6},{4,0},{6,2},{1,5},{3,7},{5,1},{7,3},{8,12},{10,14},{12... | collective-permute-start | bytes 393224 | tf_op jit(solution)/shard_map/ppermute | solution.py:317
  61.2 9.6 %collective-permute-start.12 = (bf16[4,16,8,128]{3,2,1,0:T(8,128)(2,1)S(1)}, bf16[4,16,8,128]{3,2,1,0:T(8,128)(2,1)S(1)}, u32[]{:S(2)}, u32[]{:S(2)}) collective-permute-start(bf16[4,16,8,128]{3,2,1,0:T(8,128)(2,1)S(1)} %get-tuple-element.46), channel_id=1, source_target_pairs={{0,6},{2,0},{4,2},{6,4},{1,7},{3,1},{5,3},{7,5},{8,14},{10,8},{12,... | collective-permute-start | bytes 393224 | tf_op jit(solution)/shard_map/ppermute | solution.py:317

commit v4 on v3

--- a/solution.py
+++ b/solution.py
@@ -183,15 +183,13 @@
         out_ref[:, z] = tile[...].reshape(4, SUB, SUB, LANES).astype(BF16)
 
 
-def main_frames(gain_ref, low_ref, mid_ref, coef_ref, table_ref, out_ref, frames, rows, spec, tiles, held, sem):
+def main_frames(gain_ref, v_ref, coef_ref, table_ref, out_ref, frames, rows, spec, tiles, held, sem):
     step = pl.program_id(0)
     fetch = pltpu.make_async_copy(table_ref, held, sem)
     pl.when(step == 0)(fetch.start)
 
     def load(frame, low):
-        if frame < 8:
-            return low_ref[:, pl.ds(low + frame * NFFT, LANES)]
-        return mid_ref[:, pl.ds(low + (frame - 8) * NFFT, LANES)]
+        return v_ref[:, pl.ds(low + frame * NFFT, LANES)]
 
     def emit(s, j, total, diff):
         at = pl.ds(pl.multiple_of(s * 64 + 16 * step, 16), 16)
@@ -262,7 +260,7 @@
                 out_ref[((ysrc * RING + zsrc) * 4 + xsrc) * 2 + source_core] = ref[dy, k]
 
 
-def correlate(scale, main_ref, last_ref, out_ref, left, swap):
+def correlate(scale, main_ref, last_ref, out_ref, left, swap, corner):
     item = pl.program_id(0)
     block = pl.program_id(1)
     half = DEVICES // 2
@@ -296,12 +294,25 @@
         pl.when((block == 0) & (item == which))(functools.partial(collect, which))
 
     count = out_ref.shape[2]
-    at = pl.ds(pl.multiple_of(block * count, count), count)
-    for kind, source in enumerate((left, swap)):
-        product = lax.dot_general(
-            source[at, :], left[...], (((1,), (1,)), ((), ())), preferred_element_type=F32
-        )
-        out_ref[0, kind] = (product * scale).astype(BF16)
+
+    @pl.when(block == 0)
+    def _():
+        for kind, source in enumerate((left, swap)):
+            product = scale * lax.dot_general(
+                source[:count, :], left[...], (((1,), (1,)), ((), ())), preferred_element_type=F32
+            )
+            out_ref[0, kind] = product.astype(BF16)
+            corner[kind] = product[:, count:]
+
+    @pl.when(block == 1)
+    def _():
+        for kind, source in enumerate((left, swap)):
+            product = scale * lax.dot_general(
+                source[count:, :], left[count:, :], (((1,), (1,)), ((), ())), preferred_element_type=F32
+            )
+            out_ref[0, kind, :, count:] = product.astype(BF16)
+            turned = corner[kind].T
+            out_ref[0, kind, :, :count] = (-turned if kind else turned).astype(BF16)
 
 
 def along_ring(block, distance):
@@ -388,9 +399,7 @@
     main = call(
         main_frames, (BLKS // 2,),
         [
-            SMEM,
-            pl.BlockSpec((16, 2 * quarter), lambda g: (g, 0)),
-            pl.BlockSpec((16, quarter), lambda g: (g, 2)),
+            SMEM, pl.BlockSpec((16, samples), lambda g: (g, 0)),
         ] + tables,
         IN_VMEM, pltpu.VMEM((3,) + owners, BF16),
         [
@@ -399,14 +408,14 @@
             pltpu.VMEM((4, DEVICES, 768), F32),
             pltpu.VMEM((3 * RING, FLAT * SUB, LANES), F32),
         ] + table_scratch,
-        "main_frames", 52,
-    )(main_gains, stream, stream, coefs, table)
-    ring, far, tail, main = lax.optimization_barrier((ring, far, tail, main))
+        "main_frames", 38,
+    )(main_gains, stream, coefs, table)
     packed = (DEVICES, 3) + tile
     main = pl.pallas_call(
         complete, in_specs=[IN_VMEM] * 2, out_specs=IN_VMEM, out_shape=pltpu.VMEM(packed, BF16), name="complete",
         compiler_params=pltpu.CompilerParams(vmem_limit_bytes=8 * MIB),
     )(in_vmem(main.reshape((3, DEVICES) + tile)), in_vmem(tail.reshape((DEVICES,) + tile)))
+    far, ring, main = lax.optimization_barrier((far, ring, main))
     main = lax.all_to_all(main, AXES, split_axis=0, concat_axis=0, tiled=True)
 
     leaving = jnp.stack([lax.dynamic_index_in_dim(a, 1 - core[0], 0, keepdims=False) for a in ring])
@@ -420,13 +429,13 @@
     last, = simple(arrange, (y, z, x, core), by_x, [(DEVICES,) + tile], "arrange")
 
     scale = 1.0 / (BLKS * SPEC * lax.axis_size("yh"))
-    block = 512
+    block = inputs // 2
     return call(
-        functools.partial(correlate, scale), (2, inputs // block),
+        functools.partial(correlate, scale), (2, 2),
         [whole(*packed), whole(DEVICES, *tile)],
         pl.BlockSpec((1, 2, block, inputs), lambda m, r: (m, 0, r, 0)),
         jax.ShapeDtypeStruct((2, 2, inputs, inputs), BF16),
-        [pltpu.VMEM((inputs, 4 * LANES), BF16), pltpu.VMEM((inputs, 4 * LANES), BF16)],
+        [pltpu.VMEM((inputs, 4 * LANES), BF16)] * 2 + [pltpu.VMEM((2, block, block), F32)],
         "correlate", 28,
     )(main, last)
 

time: 92.1 us -> 90.7 us (0.985)
  Pallas kernels: 23.9 us -> 22.8 us
    pallas_call x2, Pallas kernels: 15.7 us -> 13.9 us  [the longest x1 7.14 us: on_device(): call(functools.partial(correlate, scale), (2, 2), [whole(*packed), whole(...]
  transfers between devices with their start and end apart: 14 -> 14, of which waited for: 8 -> 8; matrix products, arithmetic and copies ran while one was open for 0% -> 0% of each run, Pallas kernels for 9% -> 10%
where the time goes in v4:
time: 90.7 us; the launch traced here: 90.6 us
  starting transfers between devices  35.1 us (39%)
  waiting for transfers between devices  32.2 us (36%)
  Pallas kernels  22.8 us (25%)
    ppermute x9, waiting for transfers between devices, along(): lax.ppermute(block, axis, [(i, (i + distance) % size) for i in range(size)])  19.2 us
    ppermute x9, starting transfers between devices, along(): lax.ppermute(block, axis, [(i, (i + distance) % size) for i in range(size)])  14 us
    all_to_all x1, waiting for transfers between devices, on_device(): main = lax.all_to_all(main, AXES, split_axis=0, concat_axis=0, tiled=True)  13.1 us
    ppermute x4, starting transfers between devices, along_ring(): return lax.ppermute(block, ('z', 'c'), route)  12 us
    all_to_all x1, starting transfers between devices, on_device(): main = lax.all_to_all(main, AXES, split_axis=0, concat_axis=0, tiled=True)  9.16 us
    pallas_call x1, Pallas kernels, on_device(): call(functools.partial(correlate, scale), (2, 2), [whole(*packed), whole(...  7.14 us
    pallas_call x1, Pallas kernels, on_device(): call(last_frames, (BLKS // 2,), [SMEM, SMEM, SMEM, SMEM, pl.BlockSpec((16...  7.06 us
    pallas_call x1, Pallas kernels, on_device(): call(main_frames, (BLKS // 2,), [SMEM, pl.BlockSpec((16, samples), lambda...  6.79 us
  transfers between devices with their start and end apart: 14, of which 8 were waited for; matrix products, arithmetic and copies ran while one was open for 0% of the time, Pallas kernels for 10%

profile of v4, /device:TPU:1, one launch (start us, length us, event | category | flops | bytes accessed | tf_op | source)
XLA Modules:
  0.0 90.6 jit_solution(13151714721423393077)
XLA Ops:
  0.0 0.0 copy-start
  0.0 0.0 copy-start.1
  0.0 0.0 copy-start.2
  0.0 0.0 copy-start.3
  0.0 7.1 %last_frames.1 = (bf16[3,2,16,8,128]{4,3,2,1,0:T(8,128)(2,1)S(1)}, bf16[4,2,16,8,128]{4,3,2,1,0:T(8,128)(2,1)S(1)}, bf16[16,8,128]{2,1,0:T(8,128)(2,1)S(1)}, bf1...) custom-call(s32[1]{0:T(128)} %bitcast.y_ref, s32[1]{0:T(128)} %bitcast.1.z_ref, s32[1]{0:T(128)} %bitcast.2.c_ref, ...), custom_call_target="tpu_custom_call" | custom-call | tf_op jit(solution)/shard_map/last_frames/pallas_call | solution.py:376
  7.1 3.3 %collective-permute-start = (bf16[4,2,16,8,128]{4,3,2,1,0:T(8,128)(2,1)S(1)}, bf16[4,2,16,8,128]{4,3,2,1,0:T(8,128)(2,1)S(1)}, u32[]{:S(2)}, u32[]{:S(2)}) collective-permute-start(bf16[4,2,16,8,128]{4,3,2,1,0:T(8,128)(2,1)S(1)} %get-tuple-element.26), channel_id=1, source_target_pairs={{0,1},{1,0},{2,3},{3,2},{4,5},{5,4},{6,7},{7,6},{8,9},{9,8},{10,11... | collective-permute-start | bytes 786440 | tf_op jit(solution)/shard_map/ppermute | solution.py:328
  10.4 1.2 %collective-permute-start.5 = (bf16[4,8,8,8,128]{4,3,2,1,0:T(8,128)(2,1)S(1)}, bf16[4,8,8,8,128]{4,3,2,1,0:T(8,128)(2,1)S(1)}, u32[]{:S(2)}, u32[]{:S(2)}) collective-permute-start(bf16[4,8,8,8,128]{4,3,2,1,0:T(8,128)(2,1)S(1)} %get-tuple-element.30), channel_id=1, source_target_pairs={{0,128},{128,0},{1,129},{129,1},{2,130},{130,2},{3,131},{131,3},{4... | collective-permute-start | bytes 1572872 | tf_op jit(solution)/shard_map/ppermute | solution.py:328
  11.6 0.0 collective-permute-done
  11.7 5.7 %collective-permute-start.2 = (bf16[2,2,16,8,128]{4,3,2,0,1:T(8,128)(2,1)S(1)}, bf16[2,2,16,8,128]{4,3,2,0,1:T(8,128)(2,1)S(1)}, u32[]{:S(2)}, u32[]{:S(2)}) collective-permute-start(bf16[2,2,16,8,128]{4,3,2,0,1:T(8,128)(2,1)S(1)} %pad_maximum_fusion.1), channel_id=1, source_target_pairs={{0,8},{1,57},{8,16},{9,1},{16,24},{17,9},{24,32},{25,17},{32,40},{... | collective-permute-start | bytes 393224 | tf_op jit(solution)/shard_map/ppermute | solution.py:324
  17.4 1.3 %collective-permute-start.3 = (bf16[2,2,16,8,128]{4,3,2,0,1:T(8,128)(2,1)S(1)}, bf16[2,2,16,8,128]{4,3,2,0,1:T(8,128)(2,1)S(1)}, u32[]{:S(2)}, u32[]{:S(2)}) collective-permute-start(bf16[2,2,16,8,128]{4,3,2,0,1:T(8,128)(2,1)S(1)} %pad_maximum_fusion.2), channel_id=1, source_target_pairs={{0,16},{1,49},{8,24},{9,57},{16,32},{17,1},{24,40},{25,9},{32,48},... | collective-permute-start | bytes 393224 | tf_op jit(solution)/shard_map/ppermute | solution.py:324
  18.6 0.5 collective-permute-start.4
  19.2 4.6 %collective-permute-start.1 = (bf16[2,16,8,128]{3,2,1,0:T(8,128)(2,1)S(1)}, bf16[2,16,8,128]{3,2,1,0:T(8,128)(2,1)S(1)}, u32[]{:S(2)}, u32[]{:S(2)}) collective-permute-start(bf16[2,16,8,128]{3,2,1,0:T(8,128)(2,1)S(1)} %pad_maximum_fusion.4), channel_id=1, source_target_pairs={{0,32},{1,33},{8,40},{9,41},{16,48},{17,49},{24,56},{25,57},{32,0}... | collective-permute-start | bytes 196616 | tf_op jit(solution)/shard_map/ppermute | solution.py:324
  23.7 0.0 copy-done
  23.7 0.0 copy-done.1
  23.7 0.0 copy-done.2
  23.7 0.0 copy-done.3
  23.7 6.8 %main_frames.1 = bf16[3,4,8,8,8,128]{5,4,3,2,1,0:T(8,128)(2,1)S(1)} custom-call(f32[8]{0:T(128)S(1)} %copy-done.3, bf16[64,32768]{1,0:T(8,128)(2,1)S(1)} %bitcast.26, f32[4,2048]{1,0:T(4,128)S(1)} %copy-done.2, bf16[4,256,1024]{2,1,0:T(8,128)(2,1)S(1)} %copy-done.1), custom_call_target="tpu_custom_call" | custom-call | tf_op jit(solution)/shard_map/main_frames/pallas_call | solution.py:399
  30.5 0.0 collective-permute-done.5
  30.6 1.4 %complete.1 = bf16[256,3,8,128]{3,2,1,0:T(8,128)(2,1)} custom-call(bf16[3,256,8,128]{3,2,1,0:T(8,128)(2,1)S(1)} %bitcast.27, bf16[256,8,128]{2,1,0:T(8,128)(2,1)S(1)} %bitcast.28), custom_call_target="tpu_custom_call" | custom-call | tf_op jit(solution)/shard_map/complete/pallas_call | solution.py:414
  32.0 0.0 collective-permute-done.1.far_ref
  32.0 0.0 collective-permute-done.2
  32.0 0.0 collective-permute-done.3
  32.0 0.0 collective-permute-done.4
  32.0 9.2 %all-to-all-start = ((bf16[256,3,8,128]{3,2,1,0:T(8,128)(2,1)}), bf16[256,3,8,128]{3,2,1,0:T(8,128)(2,1)S(1)}, u32[]{:S(2)}, u32[]{:S(2)}) async-start(bf16[256,3,8,128]{3,2,1,0:T(8,128)(2,1)} %complete.1), calls=%async_computation | async-start | bytes 3145728 | tf_op jit(solution)/shard_map/all_to_all | solution.py:419
  41.3 2.2 %collective-permute-start.6 = (bf16[3,2,16,8,128]{4,3,2,0,1:T(8,128)(2,1)S(1)}, bf16[3,2,16,8,128]{4,3,2,0,1:T(8,128)(2,1)S(1)}, u32[]{:S(2)}, u32[]{:S(2)}) collective-permute-start(bf16[3,2,16,8,128]{4,3,2,0,1:T(8,128)(2,1)S(1)} %pad_maximum_fusion), channel_id=1, source_target_pairs={{0,1},{1,0},{2,3},{3,2},{4,5},{5,4},{6,7},{7,6},{8,9},{9,8},{10,11... | collective-permute-start | bytes 589832 | tf_op jit(solution)/shard_map/ppermute | solution.py:328
  43.5 1.0 %collective-permute-done.6 = bf16[3,2,16,8,128]{4,3,2,0,1:T(8,128)(2,1)S(1)} collective-permute-done((bf16[3,2,16,8,128]{4,3,2,0,1:T(8,128)(2,1)S(1)}, bf16[3,2,16,8,128]{4,3,2,0,1:T(8,128)(2,1)S(1)}, u32[]{:S(2)}, u32[]{:S(2)}) %collective-permute-start.6) | collective-permute-done | bytes 196640 | tf_op jit(solution)/shard_map/ppermute | solution.py:328
  44.6 0.1 collective-permute-start.7
  44.7 2.0 %collective-permute-start.8 = (bf16[16,4,8,128]{3,2,1,0:T(8,128)(2,1)S(1)}, bf16[16,4,8,128]{3,2,1,0:T(8,128)(2,1)S(1)}, u32[]{:S(2)}, u32[]{:S(2)}) collective-permute-start(bf16[16,4,8,128]{3,2,1,0:T(8,128)(2,1)S(1)} %get-tuple-element.39), channel_id=1, source_target_pairs={{0,128},{64,192},{128,0},{192,64},{1,129},{65,193},{129,1},{193,65... | collective-permute-start | bytes 393224 | tf_op jit(solution)/shard_map/ppermute | solution.py:328
  46.8 1.1 %collective-permute-start.9 = (bf16[16,4,8,128]{3,2,1,0:T(8,128)(2,1)S(1)}, bf16[16,4,8,128]{3,2,1,0:T(8,128)(2,1)S(1)}, u32[]{:S(2)}, u32[]{:S(2)}) collective-permute-start(bf16[16,4,8,128]{3,2,1,0:T(8,128)(2,1)S(1)} %get-tuple-element.40), channel_id=1, source_target_pairs={{0,192},{64,0},{128,64},{192,128},{1,193},{65,1},{129,65},{193,129... | collective-permute-start | bytes 393224 | tf_op jit(solution)/shard_map/ppermute | solution.py:328
  47.9 5.5 %collective-permute-done.7.a1_ref = bf16[16,4,8,128]{3,2,1,0:T(8,128)(2,1)S(1)} collective-permute-done((bf16[16,4,8,128]{3,2,1,0:T(8,128)(2,1)S(1)}, bf16[16,4,8,128]{3,2,1,0:T(8,128)(2,1)S(1)}, u32[]{:S(2)}, u32[]{:S(2)}) %collective-permute-start.7) | collective-permute-done | bytes 131104 | tf_op jit(solution)/shard_map/ppermute | solution.py:328
  53.4 3.3 %collective-permute-done.8.a2_ref = bf16[16,4,8,128]{3,2,1,0:T(8,128)(2,1)S(1)} collective-permute-done((bf16[16,4,8,128]{3,2,1,0:T(8,128)(2,1)S(1)}, bf16[16,4,8,128]{3,2,1,0:T(8,128)(2,1)S(1)}, u32[]{:S(2)}, u32[]{:S(2)}) %collective-permute-start.8) | collective-permute-done | bytes 131104 | tf_op jit(solution)/shard_map/ppermute | solution.py:328
  56.7 1.1 %collective-permute-done.9.a3_ref = bf16[16,4,8,128]{3,2,1,0:T(8,128)(2,1)S(1)} collective-permute-done((bf16[16,4,8,128]{3,2,1,0:T(8,128)(2,1)S(1)}, bf16[16,4,8,128]{3,2,1,0:T(8,128)(2,1)S(1)}, u32[]{:S(2)}, u32[]{:S(2)}) %collective-permute-start.9) | collective-permute-done | bytes 131104 | tf_op jit(solution)/shard_map/ppermute | solution.py:328
  57.8 0.1 sort_x.1
  57.9 0.2 collective-permute-start.10
  58.1 2.4 %collective-permute-start.11 = (bf16[4,16,8,128]{3,2,1,0:T(8,128)(2,1)S(1)}, bf16[4,16,8,128]{3,2,1,0:T(8,128)(2,1)S(1)}, u32[]{:S(2)}, u32[]{:S(2)}) collective-permute-start(bf16[4,16,8,128]{3,2,1,0:T(8,128)(2,1)S(1)} %get-tuple-element.43), channel_id=1, source_target_pairs={{0,4},{2,6},{4,0},{6,2},{1,5},{3,7},{5,1},{7,3},{8,12},{10,14},{12... | collective-permute-start | bytes 393224 | tf_op jit(solution)/shard_map/ppermute | solution.py:328
  60.5 1.3 %collective-permute-start.12 = (bf16[4,16,8,128]{3,2,1,0:T(8,128)(2,1)S(1)}, bf16[4,16,8,128]{3,2,1,0:T(8,128)(2,1)S(1)}, u32[]{:S(2)}, u32[]{:S(2)}) collective-permute-start(bf16[4,16,8,128]{3,2,1,0:T(8,128)(2,1)S(1)} %get-tuple-element.44), channel_id=1, source_target_pairs={{0,6},{2,0},{4,2},{6,4},{1,7},{3,1},{5,3},{7,5},{8,14},{10,8},{12,... | collective-permute-start | bytes 393224 | tf_op jit(solution)/shard_map/ppermute | solution.py:328
  61.9 2.6 %collective-permute-done.10.a1_ref = bf16[4,16,8,128]{3,2,1,0:T(8,128)(2,1)S(1)} collective-permute-done((bf16[4,16,8,128]{3,2,1,0:T(8,128)(2,1)S(1)}, bf16[4,16,8,128]{3,2,1,0:T(8,128)(2,1)S(1)}, u32[]{:S(2)}, u32[]{:S(2)}) %collective-permute-start.10) | collective-permute-done | bytes 131104 | tf_op jit(solution)/shard_map/ppermute | solution.py:328
  64.5 5.0 %collective-permute-done.11.a2_ref = bf16[4,16,8,128]{3,2,1,0:T(8,128)(2,1)S(1)} collective-permute-done((bf16[4,16,8,128]{3,2,1,0:T(8,128)(2,1)S(1)}, bf16[4,16,8,128]{3,2,1,0:T(8,128)(2,1)S(1)}, u32[]{:S(2)}, u32[]{:S(2)}) %collective-permute-start.11) | collective-permute-done | bytes 131104 | tf_op jit(solution)/shard_map/ppermute | solution.py:328
  69.5 0.6 collective-permute-done.12.a3_ref
  70.1 0.3 arrange.1.last_ref
  70.3 13.1 %all-to-all-done.main_ref = bf16[256,3,8,128]{3,2,1,0:T(8,128)(2,1)S(1)} async-done(((bf16[256,3,8,128]{3,2,1,0:T(8,128)(2,1)}), bf16[256,3,8,128]{3,2,1,0:T(8,128)(2,1)S(1)}, u32[]{:S(2)}, u32[]{:S(2)}) %all-to-all-start) | async-done | bytes 1572896 | tf_op jit(solution)/shard_map/all_to_all | solution.py:419
  83.4 7.1 %correlate.1 = bf16[2,2,1024,1024]{3,2,1,0:T(8,128)(2,1)} custom-call(bf16[256,3,8,128]{3,2,1,0:T(8,128)(2,1)S(1)} %all-to-all-done.main_ref, bf16[256,8,128]{2,1,0:T(8,128)(2,1)S(1)} %arrange.1.last_ref), custom_call_target="tpu_custom_call" | custom-call | tf_op jit(solution)/shard_map/correlate/pallas_call | solution.py:433
  (15 shorter events, 0.2 us)
Async XLA Ops:
  0.0 23.7 %copy-start = (bf16[8,1,8,32768]{3,2,1,0:T(8,128)(2,1)S(1)}, bf16[8,1,8,32768]{3,2,1,0:T(8,128)(2,1)}, u32[]{:S(2)}) copy-start(bf16[8,1,8,32768]{3,2,1,0:T(8,128)(2,1)} %param.4) | copy-start | bytes 12582916
  0.0 23.7 %copy-start.1 = (bf16[4,256,1024]{2,1,0:T(8,128)(2,1)S(1)}, bf16[4,256,1024]{2,1,0:T(8,128)(2,1)}, u32[]{:S(2)}) copy-start(bf16[4,256,1024]{2,1,0:T(8,128)(2,1)} %constant.39.clone.table_ref) | copy-start | bytes 6291460
  0.0 23.7 %copy-start.2 = (f32[4,2048]{1,0:T(4,128)S(1)}, f32[4,2048]{1,0:T(4,128)}, u32[]{:S(2)}) copy-start(f32[4,2048]{1,0:T(4,128)} %constant.38.clone.coef_ref) | copy-start | bytes 98308
  0.0 23.7 %copy-start.3 = (f32[8]{0:T(128)S(1)}, f32[8]{0:T(128)}, u32[]{:S(2)}) copy-start(f32[8]{0:T(128)} %gain_ref.2) | copy-start | bytes 100
  7.1 4.5 %collective-permute-start = (bf16[4,2,16,8,128]{4,3,2,1,0:T(8,128)(2,1)S(1)}, bf16[4,2,16,8,128]{4,3,2,1,0:T(8,128)(2,1)S(1)}, u32[]{:S(2)}, u32[]{:S(2)}) collective-permute-start(bf16[4,2,16,8,128]{4,3,2,1,0:T(8,128)(2,1)S(1)} %get-tuple-element.26), channel_id=1, source_target_pairs={{0,1},{1,0},{2,3},{3,2},{4,5},{5,4},{6,7},{7,6},{8,9},{9,8},{10,11... | collective-permute-start | bytes 786440 | tf_op jit(solution)/shard_map/ppermute | solution.py:328
  10.4 20.2 %collective-permute-start.5 = (bf16[4,8,8,8,128]{4,3,2,1,0:T(8,128)(2,1)S(1)}, bf16[4,8,8,8,128]{4,3,2,1,0:T(8,128)(2,1)S(1)}, u32[]{:S(2)}, u32[]{:S(2)}) collective-permute-start(bf16[4,8,8,8,128]{4,3,2,1,0:T(8,128)(2,1)S(1)} %get-tuple-element.30), channel_id=1, source_target_pairs={{0,128},{128,0},{1,129},{129,1},{2,130},{130,2},{3,131},{131,3},{4... | collective-permute-start | bytes 1572872 | tf_op jit(solution)/shard_map/ppermute | solution.py:328
  11.7 20.3 %collective-permute-start.2 = (bf16[2,2,16,8,128]{4,3,2,0,1:T(8,128)(2,1)S(1)}, bf16[2,2,16,8,128]{4,3,2,0,1:T(8,128)(2,1)S(1)}, u32[]{:S(2)}, u32[]{:S(2)}) collective-permute-start(bf16[2,2,16,8,128]{4,3,2,0,1:T(8,128)(2,1)S(1)} %pad_maximum_fusion.1), channel_id=1, source_target_pairs={{0,8},{1,57},{8,16},{9,1},{16,24},{17,9},{24,32},{25,17},{32,40},{... | collective-permute-start | bytes 393224 | tf_op jit(solution)/shard_map/ppermute | solution.py:324
  17.4 14.6 %collective-permute-start.3 = (bf16[2,2,16,8,128]{4,3,2,0,1:T(8,128)(2,1)S(1)}, bf16[2,2,16,8,128]{4,3,2,0,1:T(8,128)(2,1)S(1)}, u32[]{:S(2)}, u32[]{:S(2)}) collective-permute-start(bf16[2,2,16,8,128]{4,3,2,0,1:T(8,128)(2,1)S(1)} %pad_maximum_fusion.2), channel_id=1, source_target_pairs={{0,16},{1,49},{8,24},{9,57},{16,32},{17,1},{24,40},{25,9},{32,48},... | collective-permute-start | bytes 393224 | tf_op jit(solution)/shard_map/ppermute | solution.py:324
  18.6 13.4 %collective-permute-start.4 = (bf16[2,2,16,8,128]{4,3,2,0,1:T(8,128)(2,1)S(1)}, bf16[2,2,16,8,128]{4,3,2,0,1:T(8,128)(2,1)S(1)}, u32[]{:S(2)}, u32[]{:S(2)}) collective-permute-start(bf16[2,2,16,8,128]{4,3,2,0,1:T(8,128)(2,1)S(1)} %pad_maximum_fusion.3), channel_id=1, source_target_pairs={{0,24},{1,41},{8,32},{9,49},{16,40},{17,57},{24,48},{25,1},{32,56}... | collective-permute-start | bytes 393224 | tf_op jit(solution)/shard_map/ppermute | solution.py:324
  19.2 12.8 %collective-permute-start.1 = (bf16[2,16,8,128]{3,2,1,0:T(8,128)(2,1)S(1)}, bf16[2,16,8,128]{3,2,1,0:T(8,128)(2,1)S(1)}, u32[]{:S(2)}, u32[]{:S(2)}) collective-permute-start(bf16[2,16,8,128]{3,2,1,0:T(8,128)(2,1)S(1)} %pad_maximum_fusion.4), channel_id=1, source_target_pairs={{0,32},{1,33},{8,40},{9,41},{16,48},{17,49},{24,56},{25,57},{32,0}... | collective-permute-start | bytes 196616 | tf_op jit(solution)/shard_map/ppermute | solution.py:324
  32.0 51.4 %all-to-all-start = ((bf16[256,3,8,128]{3,2,1,0:T(8,128)(2,1)}), bf16[256,3,8,128]{3,2,1,0:T(8,128)(2,1)S(1)}, u32[]{:S(2)}, u32[]{:S(2)}) async-start(bf16[256,3,8,128]{3,2,1,0:T(8,128)(2,1)} %complete.1), calls=%async_computation | async-start | bytes 3145728 | tf_op jit(solution)/shard_map/all_to_all | solution.py:419
  41.3 3.3 %collective-permute-start.6 = (bf16[3,2,16,8,128]{4,3,2,0,1:T(8,128)(2,1)S(1)}, bf16[3,2,16,8,128]{4,3,2,0,1:T(8,128)(2,1)S(1)}, u32[]{:S(2)}, u32[]{:S(2)}) collective-permute-start(bf16[3,2,16,8,128]{4,3,2,0,1:T(8,128)(2,1)S(1)} %pad_maximum_fusion), channel_id=1, source_target_pairs={{0,1},{1,0},{2,3},{3,2},{4,5},{5,4},{6,7},{7,6},{8,9},{9,8},{10,11... | collective-permute-start | bytes 589832 | tf_op jit(solution)/shard_map/ppermute | solution.py:328
  44.6 8.8 %collective-permute-start.7 = (bf16[16,4,8,128]{3,2,1,0:T(8,128)(2,1)S(1)}, bf16[16,4,8,128]{3,2,1,0:T(8,128)(2,1)S(1)}, u32[]{:S(2)}, u32[]{:S(2)}) collective-permute-start(bf16[16,4,8,128]{3,2,1,0:T(8,128)(2,1)S(1)} %get-tuple-element.38), channel_id=1, source_target_pairs={{0,64},{64,128},{128,192},{192,0},{1,65},{65,129},{129,193},{193,1... | collective-permute-start | bytes 393224 | tf_op jit(solution)/shard_map/ppermute | solution.py:328
  44.7 12.0 %collective-permute-start.8 = (bf16[16,4,8,128]{3,2,1,0:T(8,128)(2,1)S(1)}, bf16[16,4,8,128]{3,2,1,0:T(8,128)(2,1)S(1)}, u32[]{:S(2)}, u32[]{:S(2)}) collective-permute-start(bf16[16,4,8,128]{3,2,1,0:T(8,128)(2,1)S(1)} %get-tuple-element.39), channel_id=1, source_target_pairs={{0,128},{64,192},{128,0},{192,64},{1,129},{65,193},{129,1},{193,65... | collective-permute-start | bytes 393224 | tf_op jit(solution)/shard_map/ppermute | solution.py:328
  46.8 11.0 %collective-permute-start.9 = (bf16[16,4,8,128]{3,2,1,0:T(8,128)(2,1)S(1)}, bf16[16,4,8,128]{3,2,1,0:T(8,128)(2,1)S(1)}, u32[]{:S(2)}, u32[]{:S(2)}) collective-permute-start(bf16[16,4,8,128]{3,2,1,0:T(8,128)(2,1)S(1)} %get-tuple-element.40), channel_id=1, source_target_pairs={{0,192},{64,0},{128,64},{192,128},{1,193},{65,1},{129,65},{193,129... | collective-permute-start | bytes 393224 | tf_op jit(solution)/shard_map/ppermute | solution.py:328
  57.9 6.6 %collective-permute-start.10 = (bf16[4,16,8,128]{3,2,1,0:T(8,128)(2,1)S(1)}, bf16[4,16,8,128]{3,2,1,0:T(8,128)(2,1)S(1)}, u32[]{:S(2)}, u32[]{:S(2)}) collective-permute-start(bf16[4,16,8,128]{3,2,1,0:T(8,128)(2,1)S(1)} %get-tuple-element.42), channel_id=1, source_target_pairs={{0,2},{2,4},{4,6},{6,0},{1,3},{3,5},{5,7},{7,1},{8,10},{10,12},{12... | collective-permute-start | bytes 393224 | tf_op jit(solution)/shard_map/ppermute | solution.py:328
  58.1 11.5 %collective-permute-start.11 = (bf16[4,16,8,128]{3,2,1,0:T(8,128)(2,1)S(1)}, bf16[4,16,8,128]{3,2,1,0:T(8,128)(2,1)S(1)}, u32[]{:S(2)}, u32[]{:S(2)}) collective-permute-start(bf16[4,16,8,128]{3,2,1,0:T(8,128)(2,1)S(1)} %get-tuple-element.43), channel_id=1, source_target_pairs={{0,4},{2,6},{4,0},{6,2},{1,5},{3,7},{5,1},{7,3},{8,12},{10,14},{12... | collective-permute-start | bytes 393224 | tf_op jit(solution)/shard_map/ppermute | solution.py:328
  60.5 9.6 %collective-permute-start.12 = (bf16[4,16,8,128]{3,2,1,0:T(8,128)(2,1)S(1)}, bf16[4,16,8,128]{3,2,1,0:T(8,128)(2,1)S(1)}, u32[]{:S(2)}, u32[]{:S(2)}) collective-permute-start(bf16[4,16,8,128]{3,2,1,0:T(8,128)(2,1)S(1)} %get-tuple-element.44), channel_id=1, source_target_pairs={{0,6},{2,0},{4,2},{6,4},{1,7},{3,1},{5,3},{7,5},{8,14},{10,8},{12,... | collective-permute-start | bytes 393224 | tf_op jit(solution)/shard_map/ppermute | solution.py:328

commit v5 on v4

--- a/solution.py
+++ b/solution.py
@@ -111,7 +111,7 @@
 
 
 def last_frames(y_ref, z_ref, c_ref, gain_ref, high_ref, mid_ref, coef_ref, table_ref,
-                own_ref, other_ref, far_ref, near_ref, tail_ref, frames, extra, rows, spec, tiles, held, sem):
+                own_ref, other_ref, far_ref, near_ref, tail_ref, held, frames, extra, rows, spec, tiles, sem):
     step = pl.program_id(0)
     slot_row = pl.multiple_of(16 * step + SUB * (y_ref[0] >> 1), SUB)
     fetch = pltpu.make_async_copy(table_ref, held, sem)
@@ -183,10 +183,8 @@
         out_ref[:, z] = tile[...].reshape(4, SUB, SUB, LANES).astype(BF16)
 
 
-def main_frames(gain_ref, v_ref, coef_ref, table_ref, out_ref, frames, rows, spec, tiles, held, sem):
+def main_frames(gain_ref, v_ref, coef_ref, held, out_ref, frames, rows, spec, tiles):
     step = pl.program_id(0)
-    fetch = pltpu.make_async_copy(table_ref, held, sem)
-    pl.when(step == 0)(fetch.start)
 
     def load(frame, low):
         return v_ref[:, pl.ds(low + frame * NFFT, LANES)]
@@ -206,8 +204,6 @@
                     for j in range(HALF // LANES):
                         picked = frames[half, j, pl.ds(group * 256 + i, 32, stride=SUB), :]
                         place_rows(rows, half, group, i, j, picked)
-            if half == 0:
-                fetch.wait()
             transform(held, half, rows, spec)
         for group in range(3):
             store_owners(spec, tiles, RING * group, group, group, out_ref.at[group])
@@ -368,26 +364,26 @@
     quarter = samples // 4
     tile = (SUB, LANES)
     tables = [whole(TAPS, NFFT), pl.BlockSpec(memory_space=pl.ANY)]
-    table_scratch = [pltpu.VMEM((4, DEVICES, HALF), BF16), pltpu.SemaphoreType.DMA]
 
     slab = (FLAT // 2,) + tile
     owners = (4, RING, SUB) + tile
-    last_shapes = [(3, 2) + slab, (4, 2) + slab, slab, slab, owners]
-    own, other, far, near, tail = call(
+    last_shapes = [(3, 2) + slab, (4, 2) + slab, slab, slab, owners, (4, DEVICES, HALF)]
+    own, other, far, near, tail, held_table = call(
         last_frames, (BLKS // 2,),
         [
             SMEM, SMEM, SMEM, SMEM,
             pl.BlockSpec((16, quarter), lambda g: (g, 3)),
             pl.BlockSpec((16, quarter), lambda g: (g, 2)),
         ] + tables,
-        [IN_VMEM] * 5, [pltpu.VMEM(s, BF16) for s in last_shapes],
+        [IN_VMEM] * 6, [pltpu.VMEM(s, BF16) for s in last_shapes],
         [
             pltpu.VMEM((2, HALF // LANES, 256, LANES), F32),
             pltpu.VMEM((2, HALF // LANES, (TAPS - 1) * 80, LANES), F32),
             pltpu.VMEM((4, 512, HALF), BF16),
             pltpu.VMEM((4, DEVICES, 512), F32),
             pltpu.VMEM((16, FLAT * SUB, LANES), F32),
-        ] + table_scratch,
+            pltpu.SemaphoreType.DMA,
+        ],
         "last_frames", 56,
     )(y, z, core, input_gains, stream, stream, coefs, table)
     tail = along(tail, "yh", 1, 2)
@@ -399,17 +395,17 @@
     main = call(
         main_frames, (BLKS // 2,),
         [
-            SMEM, pl.BlockSpec((16, samples), lambda g: (g, 0)),
-        ] + tables,
+            SMEM, pl.BlockSpec((16, samples), lambda g: (g, 0)), tables[0], IN_VMEM,
+        ],
         IN_VMEM, pltpu.VMEM((3,) + owners, BF16),
         [
             pltpu.VMEM((2, HALF // LANES, 768, LANES), F32),
             pltpu.VMEM((4, 768, HALF), BF16),
             pltpu.VMEM((4, DEVICES, 768), F32),
             pltpu.VMEM((3 * RING, FLAT * SUB, LANES), F32),
-        ] + table_scratch,
+        ],
         "main_frames", 38,
-    )(main_gains, stream, coefs, table)
+    )(main_gains, stream, coefs, in_vmem(held_table))
     packed = (DEVICES, 3) + tile
     main = pl.pallas_call(
         complete, in_specs=[IN_VMEM] * 2, out_specs=IN_VMEM, out_shape=pltpu.VMEM(packed, BF16), name="complete",

time: 90.7 us -> 90.5 us (level)
  transfers between devices with their start and end apart: 14 -> 14, of which waited for: 8 -> 8; matrix products, arithmetic and copies ran while one was open for 0% -> 0% of each run, Pallas kernels for 10% -> 9%
where the time goes in v5:
time: 90.5 us; the launch traced here: 90.4 us
  starting transfers between devices  35.6 us (39%)
  waiting for transfers between devices  32.2 us (36%)
  Pallas kernels  22.1 us (24%)
    ppermute x9, waiting for transfers between devices, along(): lax.ppermute(block, axis, [(i, (i + distance) % size) for i in range(size)])  19.2 us
    ppermute x9, starting transfers between devices, along(): lax.ppermute(block, axis, [(i, (i + distance) % size) for i in range(size)])  14 us
    all_to_all x1, waiting for transfers between devices, on_device(): main = lax.all_to_all(main, AXES, split_axis=0, concat_axis=0, tiled=True)  13.1 us
    ppermute x4, starting transfers between devices, along_ring(): return lax.ppermute(block, ('z', 'c'), route)  12 us
    all_to_all x1, starting transfers between devices, on_device(): main = lax.all_to_all(main, AXES, split_axis=0, concat_axis=0, tiled=True)  9.66 us
    pallas_call x1, Pallas kernels, on_device(): call(functools.partial(correlate, scale), (2, 2), [whole(*packed), whole(...  7.14 us
    pallas_call x1, Pallas kernels, on_device(): call(last_frames, (BLKS // 2,), [SMEM, SMEM, SMEM, SMEM, pl.BlockSpec((16...  6.86 us
    pallas_call x1, Pallas kernels, on_device(): call(main_frames, (BLKS // 2,), [SMEM, pl.BlockSpec((16, samples), lambda...  6.3 us
  transfers between devices with their start and end apart: 14, of which 8 were waited for; matrix products, arithmetic and copies ran while one was open for 0% of the time, Pallas kernels for 9%

profile of v5, /device:TPU:1, one launch (start us, length us, event | category | flops | bytes accessed | tf_op | source)
XLA Modules:
  0.0 90.4 jit_solution(17464400053311721119)
XLA Ops:
  0.0 0.0 copy-start
  0.0 0.0 copy-start.1
  0.0 0.0 copy-start.2
  0.0 6.9 %last_frames.1 = (bf16[3,2,16,8,128]{4,3,2,1,0:T(8,128)(2,1)S(1)}, bf16[4,2,16,8,128]{4,3,2,1,0:T(8,128)(2,1)S(1)}, bf16[16,8,128]{2,1,0:T(8,128)(2,1)S(1)}, bf1...) custom-call(s32[1]{0:T(128)} %bitcast.y_ref, ...), custom_call_target="tpu_custom_call" | custom-call | tf_op jit(solution)/shard_map/last_frames/pallas_call | solution.py:371
  6.9 3.3 %collective-permute-start = (bf16[4,2,16,8,128]{4,3,2,1,0:T(8,128)(2,1)S(1)}, bf16[4,2,16,8,128]{4,3,2,1,0:T(8,128)(2,1)S(1)}, u32[]{:S(2)}, u32[]{:S(2)}) collective-permute-start(bf16[4,2,16,8,128]{4,3,2,1,0:T(8,128)(2,1)S(1)} %get-tuple-element.27), channel_id=1, source_target_pairs={{0,1},{1,0},{2,3},{3,2},{4,5},{5,4},{6,7},{7,6},{8,9},{9,8},{10,11... | collective-permute-start | bytes 786440 | tf_op jit(solution)/shard_map/ppermute | solution.py:324
  10.2 1.2 %collective-permute-start.5 = (bf16[4,8,8,8,128]{4,3,2,1,0:T(8,128)(2,1)S(1)}, bf16[4,8,8,8,128]{4,3,2,1,0:T(8,128)(2,1)S(1)}, u32[]{:S(2)}, u32[]{:S(2)}) collective-permute-start(bf16[4,8,8,8,128]{4,3,2,1,0:T(8,128)(2,1)S(1)} %get-tuple-element.32), channel_id=1, source_target_pairs={{0,128},{128,0},{1,129},{129,1},{2,130},{130,2},{3,131},{131,3},{4... | collective-permute-start | bytes 1572872 | tf_op jit(solution)/shard_map/ppermute | solution.py:324
  11.4 0.0 collective-permute-done
  11.5 5.7 %collective-permute-start.2 = (bf16[2,2,16,8,128]{4,3,2,0,1:T(8,128)(2,1)S(1)}, bf16[2,2,16,8,128]{4,3,2,0,1:T(8,128)(2,1)S(1)}, u32[]{:S(2)}, u32[]{:S(2)}) collective-permute-start(bf16[2,2,16,8,128]{4,3,2,0,1:T(8,128)(2,1)S(1)} %pad_maximum_fusion.1), channel_id=1, source_target_pairs={{0,8},{1,57},{8,16},{9,1},{16,24},{17,9},{24,32},{25,17},{32,40},{... | collective-permute-start | bytes 393224 | tf_op jit(solution)/shard_map/ppermute | solution.py:320
  17.1 1.2 %collective-permute-start.3 = (bf16[2,2,16,8,128]{4,3,2,0,1:T(8,128)(2,1)S(1)}, bf16[2,2,16,8,128]{4,3,2,0,1:T(8,128)(2,1)S(1)}, u32[]{:S(2)}, u32[]{:S(2)}) collective-permute-start(bf16[2,2,16,8,128]{4,3,2,0,1:T(8,128)(2,1)S(1)} %pad_maximum_fusion.2), channel_id=1, source_target_pairs={{0,16},{1,49},{8,24},{9,57},{16,32},{17,1},{24,40},{25,9},{32,48},... | collective-permute-start | bytes 393224 | tf_op jit(solution)/shard_map/ppermute | solution.py:320
  18.4 0.5 collective-permute-start.4
  19.0 4.5 %collective-permute-start.1 = (bf16[2,16,8,128]{3,2,1,0:T(8,128)(2,1)S(1)}, bf16[2,16,8,128]{3,2,1,0:T(8,128)(2,1)S(1)}, u32[]{:S(2)}, u32[]{:S(2)}) collective-permute-start(bf16[2,16,8,128]{3,2,1,0:T(8,128)(2,1)S(1)} %pad_maximum_fusion.4), channel_id=1, source_target_pairs={{0,32},{1,33},{8,40},{9,41},{16,48},{17,49},{24,56},{25,57},{32,0}... | collective-permute-start | bytes 196616 | tf_op jit(solution)/shard_map/ppermute | solution.py:320
  23.5 0.0 copy-done
  23.5 0.0 copy-done.1
  23.5 0.0 copy-done.2
  23.5 6.3 %main_frames.1 = bf16[3,4,8,8,8,128]{5,4,3,2,1,0:T(8,128)(2,1)S(1)} custom-call(f32[8]{0:T(128)S(1)} %copy-done.2, bf16[64,32768]{1,0:T(8,128)(2,1)S(1)} %bitcast.26, f32[4,2048]{1,0:T(4,128)S(1)} %copy-done.1, bf16[4,256,1024]{2,1,0:T(8,128)(2,1)S(1)} %get-tuple-element.31.held), custom_call_target="tpu_custom_call" | custom-call | tf_op jit(solution)/shard_map/main_frames/pallas_call | solution.py:395
  29.8 0.0 collective-permute-done.5
  29.8 1.4 %complete.1 = bf16[256,3,8,128]{3,2,1,0:T(8,128)(2,1)} custom-call(bf16[3,256,8,128]{3,2,1,0:T(8,128)(2,1)S(1)} %bitcast.27, bf16[256,8,128]{2,1,0:T(8,128)(2,1)S(1)} %bitcast.28), custom_call_target="tpu_custom_call" | custom-call | tf_op jit(solution)/shard_map/complete/pallas_call | solution.py:410
  31.3 0.0 collective-permute-done.1.far_ref
  31.3 0.0 collective-permute-done.2
  31.3 0.0 collective-permute-done.3
  31.3 0.0 collective-permute-done.4
  31.3 9.7 %all-to-all-start = ((bf16[256,3,8,128]{3,2,1,0:T(8,128)(2,1)}), bf16[256,3,8,128]{3,2,1,0:T(8,128)(2,1)S(1)}, u32[]{:S(2)}, u32[]{:S(2)}) async-start(bf16[256,3,8,128]{3,2,1,0:T(8,128)(2,1)} %complete.1), calls=%async_computation | async-start | bytes 3145728 | tf_op jit(solution)/shard_map/all_to_all | solution.py:415
  41.0 2.2 %collective-permute-start.6 = (bf16[3,2,16,8,128]{4,3,2,0,1:T(8,128)(2,1)S(1)}, bf16[3,2,16,8,128]{4,3,2,0,1:T(8,128)(2,1)S(1)}, u32[]{:S(2)}, u32[]{:S(2)}) collective-permute-start(bf16[3,2,16,8,128]{4,3,2,0,1:T(8,128)(2,1)S(1)} %pad_maximum_fusion), channel_id=1, source_target_pairs={{0,1},{1,0},{2,3},{3,2},{4,5},{5,4},{6,7},{7,6},{8,9},{9,8},{10,11... | collective-permute-start | bytes 589832 | tf_op jit(solution)/shard_map/ppermute | solution.py:324
  43.3 1.0 %collective-permute-done.6 = bf16[3,2,16,8,128]{4,3,2,0,1:T(8,128)(2,1)S(1)} collective-permute-done((bf16[3,2,16,8,128]{4,3,2,0,1:T(8,128)(2,1)S(1)}, bf16[3,2,16,8,128]{4,3,2,0,1:T(8,128)(2,1)S(1)}, u32[]{:S(2)}, u32[]{:S(2)}) %collective-permute-start.6) | collective-permute-done | bytes 196640 | tf_op jit(solution)/shard_map/ppermute | solution.py:324
  44.4 0.1 collective-permute-start.7
  44.5 2.0 %collective-permute-start.8 = (bf16[16,4,8,128]{3,2,1,0:T(8,128)(2,1)S(1)}, bf16[16,4,8,128]{3,2,1,0:T(8,128)(2,1)S(1)}, u32[]{:S(2)}, u32[]{:S(2)}) collective-permute-start(bf16[16,4,8,128]{3,2,1,0:T(8,128)(2,1)S(1)} %get-tuple-element.41), channel_id=1, source_target_pairs={{0,128},{64,192},{128,0},{192,64},{1,129},{65,193},{129,1},{193,65... | collective-permute-start | bytes 393224 | tf_op jit(solution)/shard_map/ppermute | solution.py:324
  46.6 1.1 %collective-permute-start.9 = (bf16[16,4,8,128]{3,2,1,0:T(8,128)(2,1)S(1)}, bf16[16,4,8,128]{3,2,1,0:T(8,128)(2,1)S(1)}, u32[]{:S(2)}, u32[]{:S(2)}) collective-permute-start(bf16[16,4,8,128]{3,2,1,0:T(8,128)(2,1)S(1)} %get-tuple-element.42), channel_id=1, source_target_pairs={{0,192},{64,0},{128,64},{192,128},{1,193},{65,1},{129,65},{193,129... | collective-permute-start | bytes 393224 | tf_op jit(solution)/shard_map/ppermute | solution.py:324
  47.7 5.5 %collective-permute-done.7.a1_ref = bf16[16,4,8,128]{3,2,1,0:T(8,128)(2,1)S(1)} collective-permute-done((bf16[16,4,8,128]{3,2,1,0:T(8,128)(2,1)S(1)}, bf16[16,4,8,128]{3,2,1,0:T(8,128)(2,1)S(1)}, u32[]{:S(2)}, u32[]{:S(2)}) %collective-permute-start.7) | collective-permute-done | bytes 131104 | tf_op jit(solution)/shard_map/ppermute | solution.py:324
  53.2 3.3 %collective-permute-done.8.a2_ref = bf16[16,4,8,128]{3,2,1,0:T(8,128)(2,1)S(1)} collective-permute-done((bf16[16,4,8,128]{3,2,1,0:T(8,128)(2,1)S(1)}, bf16[16,4,8,128]{3,2,1,0:T(8,128)(2,1)S(1)}, u32[]{:S(2)}, u32[]{:S(2)}) %collective-permute-start.8) | collective-permute-done | bytes 131104 | tf_op jit(solution)/shard_map/ppermute | solution.py:324
  56.5 1.1 %collective-permute-done.9.a3_ref = bf16[16,4,8,128]{3,2,1,0:T(8,128)(2,1)S(1)} collective-permute-done((bf16[16,4,8,128]{3,2,1,0:T(8,128)(2,1)S(1)}, bf16[16,4,8,128]{3,2,1,0:T(8,128)(2,1)S(1)}, u32[]{:S(2)}, u32[]{:S(2)}) %collective-permute-start.9) | collective-permute-done | bytes 131104 | tf_op jit(solution)/shard_map/ppermute | solution.py:324
  57.6 0.1 sort_x.1
  57.7 0.2 collective-permute-start.10
  57.8 2.4 %collective-permute-start.11 = (bf16[4,16,8,128]{3,2,1,0:T(8,128)(2,1)S(1)}, bf16[4,16,8,128]{3,2,1,0:T(8,128)(2,1)S(1)}, u32[]{:S(2)}, u32[]{:S(2)}) collective-permute-start(bf16[4,16,8,128]{3,2,1,0:T(8,128)(2,1)S(1)} %get-tuple-element.45), channel_id=1, source_target_pairs={{0,4},{2,6},{4,0},{6,2},{1,5},{3,7},{5,1},{7,3},{8,12},{10,14},{12... | collective-permute-start | bytes 393224 | tf_op jit(solution)/shard_map/ppermute | solution.py:324
  60.3 1.3 %collective-permute-start.12 = (bf16[4,16,8,128]{3,2,1,0:T(8,128)(2,1)S(1)}, bf16[4,16,8,128]{3,2,1,0:T(8,128)(2,1)S(1)}, u32[]{:S(2)}, u32[]{:S(2)}) collective-permute-start(bf16[4,16,8,128]{3,2,1,0:T(8,128)(2,1)S(1)} %get-tuple-element.46), channel_id=1, source_target_pairs={{0,6},{2,0},{4,2},{6,4},{1,7},{3,1},{5,3},{7,5},{8,14},{10,8},{12,... | collective-permute-start | bytes 393224 | tf_op jit(solution)/shard_map/ppermute | solution.py:324
  61.6 2.6 %collective-permute-done.10.a1_ref = bf16[4,16,8,128]{3,2,1,0:T(8,128)(2,1)S(1)} collective-permute-done((bf16[4,16,8,128]{3,2,1,0:T(8,128)(2,1)S(1)}, bf16[4,16,8,128]{3,2,1,0:T(8,128)(2,1)S(1)}, u32[]{:S(2)}, u32[]{:S(2)}) %collective-permute-start.10) | collective-permute-done | bytes 131104 | tf_op jit(solution)/shard_map/ppermute | solution.py:324
  64.3 5.0 %collective-permute-done.11.a2_ref = bf16[4,16,8,128]{3,2,1,0:T(8,128)(2,1)S(1)} collective-permute-done((bf16[4,16,8,128]{3,2,1,0:T(8,128)(2,1)S(1)}, bf16[4,16,8,128]{3,2,1,0:T(8,128)(2,1)S(1)}, u32[]{:S(2)}, u32[]{:S(2)}) %collective-permute-start.11) | collective-permute-done | bytes 131104 | tf_op jit(solution)/shard_map/ppermute | solution.py:324
  69.3 0.6 collective-permute-done.12.a3_ref
  69.9 0.3 arrange.1.last_ref
  70.1 13.1 %all-to-all-done.main_ref = bf16[256,3,8,128]{3,2,1,0:T(8,128)(2,1)S(1)} async-done(((bf16[256,3,8,128]{3,2,1,0:T(8,128)(2,1)}), bf16[256,3,8,128]{3,2,1,0:T(8,128)(2,1)S(1)}, u32[]{:S(2)}, u32[]{:S(2)}) %all-to-all-start) | async-done | bytes 1572896 | tf_op jit(solution)/shard_map/all_to_all | solution.py:415
  83.2 7.1 %correlate.1 = bf16[2,2,1024,1024]{3,2,1,0:T(8,128)(2,1)} custom-call(bf16[256,3,8,128]{3,2,1,0:T(8,128)(2,1)S(1)} %all-to-all-done.main_ref, bf16[256,8,128]{2,1,0:T(8,128)(2,1)S(1)} %arrange.1.last_ref), custom_call_target="tpu_custom_call" | custom-call | tf_op jit(solution)/shard_map/correlate/pallas_call | solution.py:429
  (15 shorter events, 0.2 us)
Async XLA Ops:
  0.0 23.5 %copy-start = (bf16[8,1,8,32768]{3,2,1,0:T(8,128)(2,1)S(1)}, bf16[8,1,8,32768]{3,2,1,0:T(8,128)(2,1)}, u32[]{:S(2)}) copy-start(bf16[8,1,8,32768]{3,2,1,0:T(8,128)(2,1)} %param.4) | copy-start | bytes 12582916
  0.0 23.5 %copy-start.1 = (f32[4,2048]{1,0:T(4,128)S(1)}, f32[4,2048]{1,0:T(4,128)}, u32[]{:S(2)}) copy-start(f32[4,2048]{1,0:T(4,128)} %constant.38.clone.coef_ref) | copy-start | bytes 98308
  0.0 23.5 %copy-start.2 = (f32[8]{0:T(128)S(1)}, f32[8]{0:T(128)}, u32[]{:S(2)}) copy-start(f32[8]{0:T(128)} %gain_ref.2) | copy-start | bytes 100
  6.9 4.5 %collective-permute-start = (bf16[4,2,16,8,128]{4,3,2,1,0:T(8,128)(2,1)S(1)}, bf16[4,2,16,8,128]{4,3,2,1,0:T(8,128)(2,1)S(1)}, u32[]{:S(2)}, u32[]{:S(2)}) collective-permute-start(bf16[4,2,16,8,128]{4,3,2,1,0:T(8,128)(2,1)S(1)} %get-tuple-element.27), channel_id=1, source_target_pairs={{0,1},{1,0},{2,3},{3,2},{4,5},{5,4},{6,7},{7,6},{8,9},{9,8},{10,11... | collective-permute-start | bytes 786440 | tf_op jit(solution)/shard_map/ppermute | solution.py:324
  10.2 19.6 %collective-permute-start.5 = (bf16[4,8,8,8,128]{4,3,2,1,0:T(8,128)(2,1)S(1)}, bf16[4,8,8,8,128]{4,3,2,1,0:T(8,128)(2,1)S(1)}, u32[]{:S(2)}, u32[]{:S(2)}) collective-permute-start(bf16[4,8,8,8,128]{4,3,2,1,0:T(8,128)(2,1)S(1)} %get-tuple-element.32), channel_id=1, source_target_pairs={{0,128},{128,0},{1,129},{129,1},{2,130},{130,2},{3,131},{131,3},{4... | collective-permute-start | bytes 1572872 | tf_op jit(solution)/shard_map/ppermute | solution.py:324
  11.5 19.8 %collective-permute-start.2 = (bf16[2,2,16,8,128]{4,3,2,0,1:T(8,128)(2,1)S(1)}, bf16[2,2,16,8,128]{4,3,2,0,1:T(8,128)(2,1)S(1)}, u32[]{:S(2)}, u32[]{:S(2)}) collective-permute-start(bf16[2,2,16,8,128]{4,3,2,0,1:T(8,128)(2,1)S(1)} %pad_maximum_fusion.1), channel_id=1, source_target_pairs={{0,8},{1,57},{8,16},{9,1},{16,24},{17,9},{24,32},{25,17},{32,40},{... | collective-permute-start | bytes 393224 | tf_op jit(solution)/shard_map/ppermute | solution.py:320
  17.1 14.1 %collective-permute-start.3 = (bf16[2,2,16,8,128]{4,3,2,0,1:T(8,128)(2,1)S(1)}, bf16[2,2,16,8,128]{4,3,2,0,1:T(8,128)(2,1)S(1)}, u32[]{:S(2)}, u32[]{:S(2)}) collective-permute-start(bf16[2,2,16,8,128]{4,3,2,0,1:T(8,128)(2,1)S(1)} %pad_maximum_fusion.2), channel_id=1, source_target_pairs={{0,16},{1,49},{8,24},{9,57},{16,32},{17,1},{24,40},{25,9},{32,48},... | collective-permute-start | bytes 393224 | tf_op jit(solution)/shard_map/ppermute | solution.py:320
  18.4 12.9 %collective-permute-start.4 = (bf16[2,2,16,8,128]{4,3,2,0,1:T(8,128)(2,1)S(1)}, bf16[2,2,16,8,128]{4,3,2,0,1:T(8,128)(2,1)S(1)}, u32[]{:S(2)}, u32[]{:S(2)}) collective-permute-start(bf16[2,2,16,8,128]{4,3,2,0,1:T(8,128)(2,1)S(1)} %pad_maximum_fusion.3), channel_id=1, source_target_pairs={{0,24},{1,41},{8,32},{9,49},{16,40},{17,57},{24,48},{25,1},{32,56}... | collective-permute-start | bytes 393224 | tf_op jit(solution)/shard_map/ppermute | solution.py:320
  19.0 12.3 %collective-permute-start.1 = (bf16[2,16,8,128]{3,2,1,0:T(8,128)(2,1)S(1)}, bf16[2,16,8,128]{3,2,1,0:T(8,128)(2,1)S(1)}, u32[]{:S(2)}, u32[]{:S(2)}) collective-permute-start(bf16[2,16,8,128]{3,2,1,0:T(8,128)(2,1)S(1)} %pad_maximum_fusion.4), channel_id=1, source_target_pairs={{0,32},{1,33},{8,40},{9,41},{16,48},{17,49},{24,56},{25,57},{32,0}... | collective-permute-start | bytes 196616 | tf_op jit(solution)/shard_map/ppermute | solution.py:320
  31.3 51.9 %all-to-all-start = ((bf16[256,3,8,128]{3,2,1,0:T(8,128)(2,1)}), bf16[256,3,8,128]{3,2,1,0:T(8,128)(2,1)S(1)}, u32[]{:S(2)}, u32[]{:S(2)}) async-start(bf16[256,3,8,128]{3,2,1,0:T(8,128)(2,1)} %complete.1), calls=%async_computation | async-start | bytes 3145728 | tf_op jit(solution)/shard_map/all_to_all | solution.py:415
  41.0 3.3 %collective-permute-start.6 = (bf16[3,2,16,8,128]{4,3,2,0,1:T(8,128)(2,1)S(1)}, bf16[3,2,16,8,128]{4,3,2,0,1:T(8,128)(2,1)S(1)}, u32[]{:S(2)}, u32[]{:S(2)}) collective-permute-start(bf16[3,2,16,8,128]{4,3,2,0,1:T(8,128)(2,1)S(1)} %pad_maximum_fusion), channel_id=1, source_target_pairs={{0,1},{1,0},{2,3},{3,2},{4,5},{5,4},{6,7},{7,6},{8,9},{9,8},{10,11... | collective-permute-start | bytes 589832 | tf_op jit(solution)/shard_map/ppermute | solution.py:324
  44.4 8.8 %collective-permute-start.7 = (bf16[16,4,8,128]{3,2,1,0:T(8,128)(2,1)S(1)}, bf16[16,4,8,128]{3,2,1,0:T(8,128)(2,1)S(1)}, u32[]{:S(2)}, u32[]{:S(2)}) collective-permute-start(bf16[16,4,8,128]{3,2,1,0:T(8,128)(2,1)S(1)} %get-tuple-element.40), channel_id=1, source_target_pairs={{0,64},{64,128},{128,192},{192,0},{1,65},{65,129},{129,193},{193,1... | collective-permute-start | bytes 393224 | tf_op jit(solution)/shard_map/ppermute | solution.py:324
  44.5 12.0 %collective-permute-start.8 = (bf16[16,4,8,128]{3,2,1,0:T(8,128)(2,1)S(1)}, bf16[16,4,8,128]{3,2,1,0:T(8,128)(2,1)S(1)}, u32[]{:S(2)}, u32[]{:S(2)}) collective-permute-start(bf16[16,4,8,128]{3,2,1,0:T(8,128)(2,1)S(1)} %get-tuple-element.41), channel_id=1, source_target_pairs={{0,128},{64,192},{128,0},{192,64},{1,129},{65,193},{129,1},{193,65... | collective-permute-start | bytes 393224 | tf_op jit(solution)/shard_map/ppermute | solution.py:324
  46.6 11.0 %collective-permute-start.9 = (bf16[16,4,8,128]{3,2,1,0:T(8,128)(2,1)S(1)}, bf16[16,4,8,128]{3,2,1,0:T(8,128)(2,1)S(1)}, u32[]{:S(2)}, u32[]{:S(2)}) collective-permute-start(bf16[16,4,8,128]{3,2,1,0:T(8,128)(2,1)S(1)} %get-tuple-element.42), channel_id=1, source_target_pairs={{0,192},{64,0},{128,64},{192,128},{1,193},{65,1},{129,65},{193,129... | collective-permute-start | bytes 393224 | tf_op jit(solution)/shard_map/ppermute | solution.py:324
  57.7 6.6 %collective-permute-start.10 = (bf16[4,16,8,128]{3,2,1,0:T(8,128)(2,1)S(1)}, bf16[4,16,8,128]{3,2,1,0:T(8,128)(2,1)S(1)}, u32[]{:S(2)}, u32[]{:S(2)}) collective-permute-start(bf16[4,16,8,128]{3,2,1,0:T(8,128)(2,1)S(1)} %get-tuple-element.44), channel_id=1, source_target_pairs={{0,2},{2,4},{4,6},{6,0},{1,3},{3,5},{5,7},{7,1},{8,10},{10,12},{12... | collective-permute-start | bytes 393224 | tf_op jit(solution)/shard_map/ppermute | solution.py:324
  57.8 11.5 %collective-permute-start.11 = (bf16[4,16,8,128]{3,2,1,0:T(8,128)(2,1)S(1)}, bf16[4,16,8,128]{3,2,1,0:T(8,128)(2,1)S(1)}, u32[]{:S(2)}, u32[]{:S(2)}) collective-permute-start(bf16[4,16,8,128]{3,2,1,0:T(8,128)(2,1)S(1)} %get-tuple-element.45), channel_id=1, source_target_pairs={{0,4},{2,6},{4,0},{6,2},{1,5},{3,7},{5,1},{7,3},{8,12},{10,14},{12... | collective-permute-start | bytes 393224 | tf_op jit(solution)/shard_map/ppermute | solution.py:324
  60.3 9.6 %collective-permute-start.12 = (bf16[4,16,8,128]{3,2,1,0:T(8,128)(2,1)S(1)}, bf16[4,16,8,128]{3,2,1,0:T(8,128)(2,1)S(1)}, u32[]{:S(2)}, u32[]{:S(2)}) collective-permute-start(bf16[4,16,8,128]{3,2,1,0:T(8,128)(2,1)S(1)} %get-tuple-element.46), channel_id=1, source_target_pairs={{0,6},{2,0},{4,2},{6,4},{1,7},{3,1},{5,3},{7,5},{8,14},{10,8},{12,... | collective-permute-start | bytes 393224 | tf_op jit(solution)/shard_map/ppermute | solution.py:324
